TPU v7x, 1024 devices: a whole 4x8x16 slice. The times are simulated.
1024 devices in a mesh: gx: 8 (over y_hi, x), gy: 8 (over y_lo, core), gz: 16 (over z).
Axes of the slice: x: 4, y: 8 (y_hi: 2, y_lo: 4; y = y_hi * 4 + y_lo), z: 16, core: 2. Of those that a mesh axis runs over, the one named last changes fastest.
Arguments:
- e_field: float32 [3, 64, 64, 2048], P(None, 'gx', 'gy', 'gz'), may hold values from -6 to 6
- material: int32 [64, 64, 2048], P('gx', 'gy', 'gz'), may hold values from 0 to 15
- permittivity: float32 [16], replicated, may hold values from 1 to 8
- loss: float32 [16], replicated, may hold values from 0 to 0.5
- port_cell: int32 [16384], P(('gx', 'gy', 'gz')), may hold values from 0 to 8191, as said below
- port_owner: int32 [16384, 1], P(('gx', 'gy', 'gz')), may hold values from 0 to 15; in each aligned block of 16 rows (0 to 15, 16 to 31, ...) at most 2 rows name the same one
- circuit_block: int32 [32768], P(('gx', 'gy', 'gz')), may hold values from 0 to 1
- circuit_state: float32 [32768, 256], P(('gx', 'gy', 'gz')), may hold values from -6 to 6
- mna_update: float32 [2048, 256, 256], P(('gx', 'gy', 'gz')), as said below
- mna_drive: float32 [2048, 256], P(('gx', 'gy', 'gz')), may hold values from -6 to 6
- mna_sense: float32 [2048, 256], P(('gx', 'gy', 'gz')), may hold values from -0.375 to 0.375
Outputs:
- e_final: float32 [3, 64, 64, 2048], P(None, 'gx', 'gy', 'gz')
- h_final: float32 [3, 64, 64, 2048], P(None, 'gx', 'gy', 'gz')
- circuit_final: float32 [32768, 256], P(('gx', 'gy', 'gz'))
Inputs may be any that keep to these rules, and one draw needn't show every extreme that they name: `port_cell`: the 16 ports of one device lie in distinct cells. `port_owner`: among the 16 ports of one device no owner is named more than 2 times. `mna_update`: diagonal entries of each block lie between 0.4 and 0.8; off-diagonal entries are of about 0.3/sqrt(256).
All inputs are finite; a program needn't handle non-finite values.
Results may differ from a plain program's by a relative error of at most 0.0003.
Values sent between devices are 32-bit elements; how exact they have to be, the bound alone decides.
A program may use at most 32 MiB of HBM per device.

v0:
```python
import jax
import jax.numpy as jnp
from jax import lax
from jax.sharding import PartitionSpec as P

ITERS = 4


def with_halo(block, sides, width):
    for axis, dim in sides:
        count = lax.axis_size(axis)
        forward = [(i, i + 1) for i in range(count - 1)]
        backward = [(target, source) for source, target in forward]
        low = lax.ppermute(
            lax.slice_in_dim(block, block.shape[dim] - width, None, axis=dim), axis, forward
        )
        high = lax.ppermute(lax.slice_in_dim(block, 0, width, axis=dim), axis, backward)
        block = jnp.concatenate([low, block, high], axis=dim)
    return block


def curl_forward(padded):
    base = padded[:, :-1, :-1, :-1]
    plus_x = padded[:, 1:, :-1, :-1]
    plus_y = padded[:, :-1, 1:, :-1]
    plus_z = padded[:, :-1, :-1, 1:]
    comp_x = plus_y[2] - base[2] - (plus_z[1] - base[1])
    comp_y = plus_z[0] - base[0] - (plus_x[2] - base[2])
    comp_z = plus_x[1] - base[1] - (plus_y[0] - base[0])
    return jnp.stack([comp_x, comp_y, comp_z])


def curl_backward(padded):
    base = padded[:, 1:, 1:, 1:]
    minus_x = padded[:, :-1, 1:, 1:]
    minus_y = padded[:, 1:, :-1, 1:]
    minus_z = padded[:, 1:, 1:, :-1]
    comp_x = base[2] - minus_y[2] - (base[1] - minus_z[1])
    comp_y = base[0] - minus_z[0] - (base[2] - minus_x[2])
    comp_z = base[1] - minus_x[1] - (base[0] - minus_y[0])
    return jnp.stack([comp_x, comp_y, comp_z])


def port_slots(owners, groups):
    count = owners.shape[-1]
    onehot = (owners[..., None] == jnp.arange(groups, dtype=jnp.int32)).astype(jnp.float32)
    earlier = (jnp.arange(count)[None, :] < jnp.arange(count)[:, None]).astype(jnp.float32)
    counts = jnp.einsum("pq,dqg->dpg", earlier, onehot)
    return jnp.sum(counts * onehot, axis=-1).astype(jnp.int32)


def circuit_step(state, volts, blocks, update, drive, sense):
    choose = (blocks[None, :] == jnp.arange(update.shape[0], dtype=jnp.int32)[:, None]).astype(
        jnp.float32
    )
    product = jnp.einsum("pj,bij->bpi", state, update, precision=lax.Precision.HIGHEST)
    drive_rows = jnp.dot(choose.T, drive, precision=lax.Precision.HIGHEST)
    sense_rows = jnp.dot(choose.T, sense, precision=lax.Precision.HIGHEST)
    fresh = (
        jnp.einsum("bp,bpi->pi", choose, product, precision=lax.Precision.HIGHEST)
        + drive_rows * volts[:, None]
    )
    current = jnp.sum(fresh * sense_rows, axis=1)
    return (fresh, current)


def rim_factor(length, index):
    inside = (index > 0).astype(jnp.float32)
    return jnp.where(jnp.arange(length + 1) == 0, inside, jnp.float32(1.0))


def local(
    e_field,
    material,
    permittivity,
    loss,
    port_cell,
    port_owner,
    circuit_block,
    circuit_state,
    mna_update,
    mna_drive,
    mna_sense,
):
    groups = lax.axis_size("gz")
    send_cap = circuit_state.shape[0] // groups
    cells_x, cells_y, cells_z = material.shape
    matches = material[..., None] == jnp.arange(permittivity.shape[0], dtype=jnp.int32)
    keep_table = (1.0 - loss) / (1.0 + loss)
    gain_table = 0.5 / (permittivity * (1.0 + loss))
    e_keep = jnp.sum(jnp.where(matches, keep_table, 0.0), axis=-1)
    e_gain = jnp.sum(jnp.where(matches, gain_table, 0.0), axis=-1)
    owners = port_owner[:, 0]
    slot_index = port_slots(owners[None, :], groups)[0]
    keep_mask = (
        rim_factor(cells_x, lax.axis_index("gx"))[:, None, None]
        * rim_factor(cells_y, lax.axis_index("gy"))[None, :, None]
        * rim_factor(cells_z, lax.axis_index("gz"))[None, None, :]
    )
    efield = e_field
    hfield = jnp.zeros((3, cells_x + 1, cells_y + 1, cells_z + 1), jnp.float32)
    state = circuit_state
    for iteration in range(ITERS):
        volts = efield[2].reshape(-1)[port_cell]
        outgoing = jnp.zeros((groups, send_cap), jnp.float32).at[owners, slot_index].set(volts)
        incoming = lax.all_to_all(outgoing, "gz", split_axis=0, concat_axis=0, tiled=True)
        state, current = circuit_step(
            state, incoming.reshape(-1), circuit_block, mna_update, mna_drive, mna_sense
        )
        returned = lax.all_to_all(
            current.reshape(groups, send_cap), "gz", split_axis=0, concat_axis=0, tiled=True
        )
        port_current = returned[owners, slot_index]
        padded = with_halo(efield, (("gx", 1), ("gy", 2), ("gz", 3)), 1)
        hfield = (hfield - 0.5 * curl_forward(padded)) * keep_mask
        source_z = (
            jnp.zeros((cells_x * cells_y * cells_z,), jnp.float32).at[port_cell].add(port_current)
        )
        source_z = source_z.reshape(cells_x, cells_y, cells_z)
        source = jnp.stack([jnp.zeros_like(source_z), jnp.zeros_like(source_z), source_z])
        efield = e_keep * efield + e_gain * (curl_backward(hfield) - source)
    return (efield, hfield[:, 1:, 1:, 1:], state)


def solution(mesh):
    placed = (
        P(None, "gx", "gy", "gz"),
        P("gx", "gy", "gz"),
        P(),
        P(),
        P(("gx", "gy", "gz")),
        P(("gx", "gy", "gz"), None),
        P(("gx", "gy", "gz")),
        P(("gx", "gy", "gz"), None),
        P(("gx", "gy", "gz"), None, None),
        P(("gx", "gy", "gz"), None),
        P(("gx", "gy", "gz"), None),
    )
    return jax.shard_map(
        local,
        mesh=mesh,
        in_specs=placed,
        out_specs=(
            P(None, "gx", "gy", "gz"),
            P(None, "gx", "gy", "gz"),
            P(("gx", "gy", "gz"), None),
        ),
        check_vma=False,
    )
```

profile of v0, /device:TPU:6, one launch (start us, length us, event | category | flops | bytes accessed | tf_op | source)
XLA Modules:
  0.0 271.7 jit_solution(7678034899060695891)
XLA Ops:
  4.2 9.1 %collective-permute-start = (f32[3,1,8,128]{3,2,1,0:T(8,128)S(1)}, f32[3,1,8,128]{3,2,1,0:T(8,128)S(1)}, u32[]{:S(2)}, u32[]{:S(2)}) collective-permute-start(f32[3,1,8,128]{3,2,1,0:T(8,128)S(1)} %get-tuple-element.53), channel_id=1, source_target_pairs={{0,128},{128,256},{256,384},{384,512},{512,640},{640,768},{768,896... | collective-permute-start | bytes 36872 | tf_op jit(solution)/shard_map/ppermute | solution.py:14
  17.6 18.9 %all-to-all-start = ((f32[16,1,2]{2,1,0:T(1,128)}), f32[16,1,2]{2,1,0:T(1,128)S(1)}, u32[]{:S(2)}, u32[]{:S(2)}) async-start(f32[16,1,2]{2,1,0:T(1,128)} %copy.42), calls=%async_computation | async-start | bytes 16384 | tf_op jit(solution)/shard_map/all_to_all | solution.py:106
  40.3 8.6 %all-to-all-done = f32[16,1,2]{2,1,0:T(1,128)S(1)} async-done(((f32[16,1,2]{2,1,0:T(1,128)}), f32[16,1,2]{2,1,0:T(1,128)S(1)}, u32[]{:S(2)}, u32[]{:S(2)}) %all-to-all-start) | async-done | bytes 160 | tf_op jit(solution)/shard_map/all_to_all | solution.py:106
  53.9 3.5 %all-to-all-start.1 = ((f32[16,1,2]{2,1,0:T(1,128)}), f32[16,1,2]{2,1,0:T(1,128)S(1)}, u32[]{:S(2)}, u32[]{:S(2)}) async-start(f32[16,1,2]{2,1,0:T(1,128)} %bitcast.11), calls=%async_computation.1 | async-start | bytes 16384 | tf_op jit(solution)/shard_map/all_to_all | solution.py:110
  57.6 3.8 %collective-permute-start.4 = (f32[3,10,10,1]{3,2,1,0:T(8,128)S(1)}, f32[3,10,10,1]{3,2,1,0:T(8,128)S(1)}, u32[]{:S(2)}, u32[]{:S(2)}) collective-permute-start(f32[3,10,10,1]{3,2,1,0:T(8,128)S(1)} %get-tuple-element.37), channel_id=1, source_target_pairs={{0,1},{1,2},{2,3},{3,4},{4,5},{5,6},{6,7},{7,8},{8,9},{9,10},{10,1... | collective-permute-start | bytes 3608 | tf_op jit(solution)/shard_map/ppermute | solution.py:14
  62.0 7.9 %all-to-all-done.1 = f32[16,1,2]{2,1,0:T(1,128)S(1)} async-done(((f32[16,1,2]{2,1,0:T(1,128)}), f32[16,1,2]{2,1,0:T(1,128)S(1)}, u32[]{:S(2)}, u32[]{:S(2)}) %all-to-all-start.1) | async-done | bytes 160 | tf_op jit(solution)/shard_map/all_to_all | solution.py:110
  73.0 8.4 %collective-permute-done.5 = f32[3,10,10,1]{3,2,1,0:T(8,128)S(1)} collective-permute-done((f32[3,10,10,1]{3,2,1,0:T(8,128)S(1)}, f32[3,10,10,1]{3,2,1,0:T(8,128)S(1)}, u32[]{:S(2)}, u32[]{:S(2)}) %collective-permute-start.5) | collective-permute-done | bytes 1232 | tf_op jit(solution)/shard_map/ppermute | solution.py:17
  83.7 3.9 %collective-permute-start.7 = (f32[3,1,8,128]{3,2,1,0:T(8,128)S(1)}, f32[3,1,8,128]{3,2,1,0:T(8,128)S(1)}, u32[]{:S(2)}, u32[]{:S(2)}) collective-permute-start(f32[3,1,8,128]{3,2,1,0:T(8,128)S(1)} %get-tuple-element.51), channel_id=1, source_target_pairs={{128,0},{256,128},{384,256},{512,384},{640,512},{768,640},{896,768... | collective-permute-start | bytes 36872 | tf_op jit(solution)/shard_map/ppermute | solution.py:17
  94.1 11.9 %all-to-all-done.2 = f32[16,1,2]{2,1,0:T(1,128)S(1)} async-done(((f32[16,1,2]{2,1,0:T(1,128)}), f32[16,1,2]{2,1,0:T(1,128)S(1)}, u32[]{:S(2)}, u32[]{:S(2)}) %all-to-all-start.2) | async-done | bytes 160 | tf_op jit(solution)/shard_map/all_to_all | solution.py:106
  110.3 3.5 %all-to-all-start.3 = ((f32[16,1,2]{2,1,0:T(1,128)}), f32[16,1,2]{2,1,0:T(1,128)S(1)}, u32[]{:S(2)}, u32[]{:S(2)}) async-start(f32[16,1,2]{2,1,0:T(1,128)} %bitcast.20), calls=%async_computation.3 | async-start | bytes 16384 | tf_op jit(solution)/shard_map/all_to_all | solution.py:110
  118.9 7.1 %all-to-all-done.3 = f32[16,1,2]{2,1,0:T(1,128)S(1)} async-done(((f32[16,1,2]{2,1,0:T(1,128)}), f32[16,1,2]{2,1,0:T(1,128)S(1)}, u32[]{:S(2)}, u32[]{:S(2)}) %all-to-all-start.3) | async-done | bytes 160 | tf_op jit(solution)/shard_map/all_to_all | solution.py:110
  129.2 6.4 %collective-permute-done.11 = f32[3,10,10,1]{3,2,1,0:T(8,128)S(1)} collective-permute-done((f32[3,10,10,1]{3,2,1,0:T(8,128)S(1)}, f32[3,10,10,1]{3,2,1,0:T(8,128)S(1)}, u32[]{:S(2)}, u32[]{:S(2)}) %collective-permute-start.11) | collective-permute-done | bytes 1232 | tf_op jit(solution)/shard_map/ppermute | solution.py:17
  136.0 8.0 %collective-permute-start.12 = (f32[3,1,8,128]{3,2,1,0:T(8,128)S(1)}, f32[3,1,8,128]{3,2,1,0:T(8,128)S(1)}, u32[]{:S(2)}, u32[]{:S(2)}) collective-permute-start(f32[3,1,8,128]{3,2,1,0:T(8,128)S(1)} %get-tuple-element.48), channel_id=1, source_target_pairs={{0,128},{128,256},{256,384},{384,512},{512,640},{640,768},{768,896... | collective-permute-start | bytes 36872 | tf_op jit(solution)/shard_map/ppermute | solution.py:14
  148.6 4.1 %all-to-all-start.4 = ((f32[16,1,2]{2,1,0:T(1,128)}), f32[16,1,2]{2,1,0:T(1,128)S(1)}, u32[]{:S(2)}, u32[]{:S(2)}) async-start(f32[16,1,2]{2,1,0:T(1,128)} %copy.48), calls=%async_computation.4 | async-start | bytes 16384 | tf_op jit(solution)/shard_map/all_to_all | solution.py:106
  153.1 12.1 %all-to-all-done.4 = f32[16,1,2]{2,1,0:T(1,128)S(1)} async-done(((f32[16,1,2]{2,1,0:T(1,128)}), f32[16,1,2]{2,1,0:T(1,128)S(1)}, u32[]{:S(2)}, u32[]{:S(2)}) %all-to-all-start.4) | async-done | bytes 160 | tf_op jit(solution)/shard_map/all_to_all | solution.py:106
  166.0 4.0 %collective-permute-start.14 = (f32[3,10,1,128]{3,2,1,0:T(1,128)S(1)}, f32[3,10,1,128]{3,2,1,0:T(1,128)S(1)}, u32[]{:S(2)}, u32[]{:S(2)}) collective-permute-start(f32[3,10,1,128]{3,2,1,0:T(1,128)S(1)} %get-tuple-element.40), channel_id=1, source_target_pairs={{0,16},{16,32},{32,48},{48,64},{64,80},{80,96},{96,112},{1,17},{17... | collective-permute-start | bytes 46088 | tf_op jit(solution)/shard_map/ppermute | solution.py:14
  172.2 3.5 %all-to-all-start.5 = ((f32[16,1,2]{2,1,0:T(1,128)}), f32[16,1,2]{2,1,0:T(1,128)S(1)}, u32[]{:S(2)}, u32[]{:S(2)}) async-start(f32[16,1,2]{2,1,0:T(1,128)} %bitcast.28), calls=%async_computation.5 | async-start | bytes 16384 | tf_op jit(solution)/shard_map/all_to_all | solution.py:110
  182.0 5.9 %all-to-all-done.5 = f32[16,1,2]{2,1,0:T(1,128)S(1)} async-done(((f32[16,1,2]{2,1,0:T(1,128)}), f32[16,1,2]{2,1,0:T(1,128)S(1)}, u32[]{:S(2)}, u32[]{:S(2)}) %all-to-all-start.5) | async-done | bytes 160 | tf_op jit(solution)/shard_map/all_to_all | solution.py:110
  191.1 6.4 %collective-permute-done.17 = f32[3,10,10,1]{3,2,1,0:T(8,128)S(1)} collective-permute-done((f32[3,10,10,1]{3,2,1,0:T(8,128)S(1)}, f32[3,10,10,1]{3,2,1,0:T(8,128)S(1)}, u32[]{:S(2)}, u32[]{:S(2)}) %collective-permute-start.17) | collective-permute-done | bytes 1232 | tf_op jit(solution)/shard_map/ppermute | solution.py:17
  198.0 9.7 %collective-permute-start.18 = (f32[3,1,8,128]{3,2,1,0:T(8,128)S(1)}, f32[3,1,8,128]{3,2,1,0:T(8,128)S(1)}, u32[]{:S(2)}, u32[]{:S(2)}) collective-permute-start(f32[3,1,8,128]{3,2,1,0:T(8,128)S(1)} %get-tuple-element.46), channel_id=1, source_target_pairs={{0,128},{128,256},{256,384},{384,512},{512,640},{640,768},{768,896... | collective-permute-start | bytes 36872 | tf_op jit(solution)/shard_map/ppermute | solution.py:14
  212.4 4.1 %all-to-all-start.6 = ((f32[16,1,2]{2,1,0:T(1,128)}), f32[16,1,2]{2,1,0:T(1,128)S(1)}, u32[]{:S(2)}, u32[]{:S(2)}) async-start(f32[16,1,2]{2,1,0:T(1,128)} %copy.51), calls=%async_computation.6 | async-start | bytes 16384 | tf_op jit(solution)/shard_map/all_to_all | solution.py:106
  219.3 5.3 %collective-permute-start.20 = (f32[3,10,1,128]{3,2,1,0:T(1,128)S(1)}, f32[3,10,1,128]{3,2,1,0:T(1,128)S(1)}, u32[]{:S(2)}, u32[]{:S(2)}) collective-permute-start(f32[3,10,1,128]{3,2,1,0:T(1,128)S(1)} %get-tuple-element.38), channel_id=1, source_target_pairs={{0,16},{16,32},{32,48},{48,64},{64,80},{80,96},{96,112},{1,17},{17... | collective-permute-start | bytes 46088 | tf_op jit(solution)/shard_map/ppermute | solution.py:14
  236.3 21.7 %all_to_all.84 = f32[16,1,2]{2,1,0:T(1,128)S(1)} all-to-all(f32[16,1,2]{2,1,0:T(1,128)S(1)} %bitcast.125), channel_id=1, replica_groups=mesh['gx'=8,'gy'=8,'gz'=16] {'gz'}, dimensions={0} | all-to-all | bytes 256 | tf_op jit(solution)/shard_map/all_to_all | solution.py:110
  261.1 8.8 %collective-permute-done.23 = f32[3,10,10,1]{3,2,1,0:T(8,128)S(1)} collective-permute-done((f32[3,10,10,1]{3,2,1,0:T(8,128)S(1)}, f32[3,10,10,1]{3,2,1,0:T(8,128)S(1)}, u32[]{:S(2)}, u32[]{:S(2)}) %collective-permute-start.23) | collective-permute-done | bytes 1232 | tf_op jit(solution)/shard_map/ppermute | solution.py:17
  (176 shorter events, 83.5 us)
Async XLA Ops:
  1.4 48.8 %collective-permute-start.1 = (f32[3,1,8,128]{3,2,1,0:T(8,128)S(1)}, f32[3,1,8,128]{3,2,1,0:T(8,128)S(1)}, u32[]{:S(2)}, u32[]{:S(2)}) collective-permute-start(f32[3,1,8,128]{3,2,1,0:T(8,128)S(1)} %get-tuple-element.52), channel_id=1, source_target_pairs={{128,0},{256,128},{384,256},{512,384},{640,512},{768,640},{896,768... | collective-permute-start | bytes 36872 | tf_op jit(solution)/shard_map/ppermute | solution.py:17
  4.2 46.0 %collective-permute-start = (f32[3,1,8,128]{3,2,1,0:T(8,128)S(1)}, f32[3,1,8,128]{3,2,1,0:T(8,128)S(1)}, u32[]{:S(2)}, u32[]{:S(2)}) collective-permute-start(f32[3,1,8,128]{3,2,1,0:T(8,128)S(1)} %get-tuple-element.53), channel_id=1, source_target_pairs={{0,128},{128,256},{256,384},{384,512},{512,640},{640,768},{768,896... | collective-permute-start | bytes 36872 | tf_op jit(solution)/shard_map/ppermute | solution.py:14
  17.6 31.2 %all-to-all-start = ((f32[16,1,2]{2,1,0:T(1,128)}), f32[16,1,2]{2,1,0:T(1,128)S(1)}, u32[]{:S(2)}, u32[]{:S(2)}) async-start(f32[16,1,2]{2,1,0:T(1,128)} %copy.42), calls=%async_computation | async-start | bytes 16384 | tf_op jit(solution)/shard_map/all_to_all | solution.py:106
  53.9 16.0 %all-to-all-start.1 = ((f32[16,1,2]{2,1,0:T(1,128)}), f32[16,1,2]{2,1,0:T(1,128)S(1)}, u32[]{:S(2)}, u32[]{:S(2)}) async-start(f32[16,1,2]{2,1,0:T(1,128)} %bitcast.11), calls=%async_computation.1 | async-start | bytes 16384 | tf_op jit(solution)/shard_map/all_to_all | solution.py:110
  57.6 15.1 %collective-permute-start.4 = (f32[3,10,10,1]{3,2,1,0:T(8,128)S(1)}, f32[3,10,10,1]{3,2,1,0:T(8,128)S(1)}, u32[]{:S(2)}, u32[]{:S(2)}) collective-permute-start(f32[3,10,10,1]{3,2,1,0:T(8,128)S(1)} %get-tuple-element.37), channel_id=1, source_target_pairs={{0,1},{1,2},{2,3},{3,4},{4,5},{5,6},{6,7},{7,8},{8,9},{9,10},{10,1... | collective-permute-start | bytes 3608 | tf_op jit(solution)/shard_map/ppermute | solution.py:14
  71.4 10.0 %collective-permute-start.5 = (f32[3,10,10,1]{3,2,1,0:T(8,128)S(1)}, f32[3,10,10,1]{3,2,1,0:T(8,128)S(1)}, u32[]{:S(2)}, u32[]{:S(2)}) collective-permute-start(f32[3,10,10,1]{3,2,1,0:T(8,128)S(1)} %get-tuple-element.36), channel_id=1, source_target_pairs={{1,0},{2,1},{3,2},{4,3},{5,4},{6,5},{7,6},{8,7},{9,8},{10,9},{11,1... | collective-permute-start | bytes 3608 | tf_op jit(solution)/shard_map/ppermute | solution.py:17
  81.8 25.0 %collective-permute-start.6 = (f32[3,1,8,128]{3,2,1,0:T(8,128)S(1)}, f32[3,1,8,128]{3,2,1,0:T(8,128)S(1)}, u32[]{:S(2)}, u32[]{:S(2)}) collective-permute-start(f32[3,1,8,128]{3,2,1,0:T(8,128)S(1)} %get-tuple-element.50), channel_id=1, source_target_pairs={{0,128},{128,256},{256,384},{384,512},{512,640},{640,768},{768,896... | collective-permute-start | bytes 36872 | tf_op jit(solution)/shard_map/ppermute | solution.py:14
  83.7 23.0 %collective-permute-start.7 = (f32[3,1,8,128]{3,2,1,0:T(8,128)S(1)}, f32[3,1,8,128]{3,2,1,0:T(8,128)S(1)}, u32[]{:S(2)}, u32[]{:S(2)}) collective-permute-start(f32[3,1,8,128]{3,2,1,0:T(8,128)S(1)} %get-tuple-element.51), channel_id=1, source_target_pairs={{128,0},{256,128},{384,256},{512,384},{640,512},{768,640},{896,768... | collective-permute-start | bytes 36872 | tf_op jit(solution)/shard_map/ppermute | solution.py:17
  90.3 15.7 %all-to-all-start.2 = ((f32[16,1,2]{2,1,0:T(1,128)}), f32[16,1,2]{2,1,0:T(1,128)S(1)}, u32[]{:S(2)}, u32[]{:S(2)}) async-start(f32[16,1,2]{2,1,0:T(1,128)} %copy.45), calls=%async_computation.2 | async-start | bytes 16384 | tf_op jit(solution)/shard_map/all_to_all | solution.py:106
  110.3 15.8 %all-to-all-start.3 = ((f32[16,1,2]{2,1,0:T(1,128)}), f32[16,1,2]{2,1,0:T(1,128)S(1)}, u32[]{:S(2)}, u32[]{:S(2)}) async-start(f32[16,1,2]{2,1,0:T(1,128)} %bitcast.20), calls=%async_computation.3 | async-start | bytes 16384 | tf_op jit(solution)/shard_map/all_to_all | solution.py:110
  115.8 13.0 %collective-permute-start.10 = (f32[3,10,10,1]{3,2,1,0:T(8,128)S(1)}, f32[3,10,10,1]{3,2,1,0:T(8,128)S(1)}, u32[]{:S(2)}, u32[]{:S(2)}) collective-permute-start(f32[3,10,10,1]{3,2,1,0:T(8,128)S(1)} %get-tuple-element.35), channel_id=1, source_target_pairs={{0,1},{1,2},{2,3},{3,4},{4,5},{5,6},{6,7},{7,8},{8,9},{9,10},{10,1... | collective-permute-start | bytes 3608 | tf_op jit(solution)/shard_map/ppermute | solution.py:14
  136.0 29.9 %collective-permute-start.12 = (f32[3,1,8,128]{3,2,1,0:T(8,128)S(1)}, f32[3,1,8,128]{3,2,1,0:T(8,128)S(1)}, u32[]{:S(2)}, u32[]{:S(2)}) collective-permute-start(f32[3,1,8,128]{3,2,1,0:T(8,128)S(1)} %get-tuple-element.48), channel_id=1, source_target_pairs={{0,128},{128,256},{256,384},{384,512},{512,640},{640,768},{768,896... | collective-permute-start | bytes 36872 | tf_op jit(solution)/shard_map/ppermute | solution.py:14
  144.1 21.9 %collective-permute-start.13 = (f32[3,1,8,128]{3,2,1,0:T(8,128)S(1)}, f32[3,1,8,128]{3,2,1,0:T(8,128)S(1)}, u32[]{:S(2)}, u32[]{:S(2)}) collective-permute-start(f32[3,1,8,128]{3,2,1,0:T(8,128)S(1)} %get-tuple-element.49), channel_id=1, source_target_pairs={{128,0},{256,128},{384,256},{512,384},{640,512},{768,640},{896,768... | collective-permute-start | bytes 36872 | tf_op jit(solution)/shard_map/ppermute | solution.py:17
  148.6 16.5 %all-to-all-start.4 = ((f32[16,1,2]{2,1,0:T(1,128)}), f32[16,1,2]{2,1,0:T(1,128)S(1)}, u32[]{:S(2)}, u32[]{:S(2)}) async-start(f32[16,1,2]{2,1,0:T(1,128)} %copy.48), calls=%async_computation.4 | async-start | bytes 16384 | tf_op jit(solution)/shard_map/all_to_all | solution.py:106
  166.0 9.7 %collective-permute-start.14 = (f32[3,10,1,128]{3,2,1,0:T(1,128)S(1)}, f32[3,10,1,128]{3,2,1,0:T(1,128)S(1)}, u32[]{:S(2)}, u32[]{:S(2)}) collective-permute-start(f32[3,10,1,128]{3,2,1,0:T(1,128)S(1)} %get-tuple-element.40), channel_id=1, source_target_pairs={{0,16},{16,32},{32,48},{48,64},{64,80},{80,96},{96,112},{1,17},{17... | collective-permute-start | bytes 46088 | tf_op jit(solution)/shard_map/ppermute | solution.py:14
  170.0 8.8 %collective-permute-start.15 = (f32[3,10,1,128]{3,2,1,0:T(1,128)S(1)}, f32[3,10,1,128]{3,2,1,0:T(1,128)S(1)}, u32[]{:S(2)}, u32[]{:S(2)}) collective-permute-start(f32[3,10,1,128]{3,2,1,0:T(1,128)S(1)} %get-tuple-element.41), channel_id=1, source_target_pairs={{16,0},{32,16},{48,32},{64,48},{80,64},{96,80},{112,96},{17,1},{33... | collective-permute-start | bytes 46088 | tf_op jit(solution)/shard_map/ppermute | solution.py:17
  172.2 15.8 %all-to-all-start.5 = ((f32[16,1,2]{2,1,0:T(1,128)}), f32[16,1,2]{2,1,0:T(1,128)S(1)}, u32[]{:S(2)}, u32[]{:S(2)}) async-start(f32[16,1,2]{2,1,0:T(1,128)} %bitcast.28), calls=%async_computation.5 | async-start | bytes 16384 | tf_op jit(solution)/shard_map/all_to_all | solution.py:110
  179.0 11.7 %collective-permute-start.16 = (f32[3,10,10,1]{3,2,1,0:T(8,128)S(1)}, f32[3,10,10,1]{3,2,1,0:T(8,128)S(1)}, u32[]{:S(2)}, u32[]{:S(2)}) collective-permute-start(f32[3,10,10,1]{3,2,1,0:T(8,128)S(1)} %get-tuple-element.33), channel_id=1, source_target_pairs={{0,1},{1,2},{2,3},{3,4},{4,5},{5,6},{6,7},{7,8},{8,9},{9,10},{10,1... | collective-permute-start | bytes 3608 | tf_op jit(solution)/shard_map/ppermute | solution.py:14
  198.0 18.6 %collective-permute-start.18 = (f32[3,1,8,128]{3,2,1,0:T(8,128)S(1)}, f32[3,1,8,128]{3,2,1,0:T(8,128)S(1)}, u32[]{:S(2)}, u32[]{:S(2)}) collective-permute-start(f32[3,1,8,128]{3,2,1,0:T(8,128)S(1)} %get-tuple-element.46), channel_id=1, source_target_pairs={{0,128},{128,256},{256,384},{384,512},{512,640},{640,768},{768,896... | collective-permute-start | bytes 36872 | tf_op jit(solution)/shard_map/ppermute | solution.py:14
  207.6 11.6 %collective-permute-start.19 = (f32[3,1,8,128]{3,2,1,0:T(8,128)S(1)}, f32[3,1,8,128]{3,2,1,0:T(8,128)S(1)}, u32[]{:S(2)}, u32[]{:S(2)}) collective-permute-start(f32[3,1,8,128]{3,2,1,0:T(8,128)S(1)} %get-tuple-element.47), channel_id=1, source_target_pairs={{128,0},{256,128},{384,256},{512,384},{640,512},{768,640},{896,768... | collective-permute-start | bytes 36872 | tf_op jit(solution)/shard_map/ppermute | solution.py:17
  212.4 16.5 %all-to-all-start.6 = ((f32[16,1,2]{2,1,0:T(1,128)}), f32[16,1,2]{2,1,0:T(1,128)S(1)}, u32[]{:S(2)}, u32[]{:S(2)}) async-start(f32[16,1,2]{2,1,0:T(1,128)} %copy.51), calls=%async_computation.6 | async-start | bytes 16384 | tf_op jit(solution)/shard_map/all_to_all | solution.py:106
  219.3 10.4 %collective-permute-start.20 = (f32[3,10,1,128]{3,2,1,0:T(1,128)S(1)}, f32[3,10,1,128]{3,2,1,0:T(1,128)S(1)}, u32[]{:S(2)}, u32[]{:S(2)}) collective-permute-start(f32[3,10,1,128]{3,2,1,0:T(1,128)S(1)} %get-tuple-element.38), channel_id=1, source_target_pairs={{0,16},{16,32},{32,48},{48,64},{64,80},{80,96},{96,112},{1,17},{17... | collective-permute-start | bytes 46088 | tf_op jit(solution)/shard_map/ppermute | solution.py:14
  233.1 27.6 %collective-permute-start.22 = (f32[3,10,10,1]{3,2,1,0:T(8,128)S(1)}, f32[3,10,10,1]{3,2,1,0:T(8,128)S(1)}, u32[]{:S(2)}, u32[]{:S(2)}) collective-permute-start(f32[3,10,10,1]{3,2,1,0:T(8,128)S(1)} %get-tuple-element.31), channel_id=1, source_target_pairs={{0,1},{1,2},{2,3},{3,4},{4,5},{5,6},{6,7},{7,8},{8,9},{9,10},{10,1... | collective-permute-start | bytes 3608 | tf_op jit(solution)/shard_map/ppermute | solution.py:14
  259.4 10.5 %collective-permute-start.23 = (f32[3,10,10,1]{3,2,1,0:T(8,128)S(1)}, f32[3,10,10,1]{3,2,1,0:T(8,128)S(1)}, u32[]{:S(2)}, u32[]{:S(2)}) collective-permute-start(f32[3,10,10,1]{3,2,1,0:T(8,128)S(1)} %get-tuple-element.30), channel_id=1, source_target_pairs={{1,0},{2,1},{3,2},{4,3},{5,4},{6,5},{7,6},{8,7},{9,8},{10,9},{11,1... | collective-permute-start | bytes 3608 | tf_op jit(solution)/shard_map/ppermute | solution.py:17
  (19 other events, 120.7 us)
where the time goes:
time: 275 us; the launch traced here: 272 us
  starting transfers between devices  114 us (41%)
  waiting for transfers between devices  96.6 us (35%)
  local copies, waits for them, and re-layouts  22.2 us (8%)
  blocking collectives  21.7 us (8%)
  other arithmetic  11.1 us (4%)
  matrix products  4.8 us (2%)
    ppermute x12, starting transfers between devices, with_halo(): lax.ppermute(lax.slice_in_dim(block, block.shape[dim] - width, None, axis...  51.8 us
    ppermute x12, waiting for transfers between devices, with_halo(): lax.ppermute(lax.slice_in_dim(block, 0, width, axis=dim), axis, backward)  40.9 us
    all_to_all x4, waiting for transfers between devices, local(): lax.all_to_all(outgoing, 'gz', split_axis=0, concat_axis=0, tiled=True)  34.7 us
    all_to_all x4, starting transfers between devices, local(): lax.all_to_all(outgoing, 'gz', split_axis=0, concat_axis=0, tiled=True)  30.6 us
    all_to_all x1, blocking collectives, local(): lax.all_to_all(current.reshape(groups, send_cap), 'gz', split_axis=0, con...  21.7 us
    ppermute x12, starting transfers between devices, with_halo(): lax.ppermute(lax.slice_in_dim(block, 0, width, axis=dim), axis, backward)  21 us
    all_to_all x3, waiting for transfers between devices, local(): lax.all_to_all(current.reshape(groups, send_cap), 'gz', split_axis=0, con...  21 us
    all_to_all x3, starting transfers between devices, local(): lax.all_to_all(current.reshape(groups, send_cap), 'gz', split_axis=0, con...  10.4 us
  transfers between devices with their start and end apart: 31, of which 15 were waited for; matrix products, arithmetic and copies ran while one was open for 11% of the time, Pallas kernels for 0%

commit v1 on v0

v1 whole, which is shorter than its diff:
```python
import functools

import jax
import jax.numpy as jnp
from jax import lax
from jax.experimental import pallas as pl
from jax.experimental.pallas import tpu as pltpu
from jax.sharding import PartitionSpec as P

ITERS = 4
MESH = pl.DeviceIdType.MESH
AXES = ("gx", "gy", "gz")
F32 = jnp.float32
BF16 = jnp.bfloat16

MESSAGES = (
    ((1, 0, 0), 0, 3),
    ((-1, 0, 0), 3, 2),
    ((0, 1, 0), 5, 3),
    ((0, -1, 0), 8, 2),
    ((0, 0, 1), 10, 1),
    ((0, 0, -1), 11, 1),
    ((1, -1, 0), 12, 1),
    ((-1, 1, 0), 13, 1),
    ((1, 0, -1), 14, 1),
    ((0, 1, -1), 15, 1),
    ((0, -1, 1), 16, 1),
    ((-1, 0, 1), 17, 1),
)
TILES = 18


def iota(shape, dim):
    return lax.broadcasted_iota(jnp.int32, shape, dim)


def full(row):
    return jnp.broadcast_to(row, (8, 128))


def split(value, parts):
    pieces = []
    for _ in range(parts):
        piece = value.astype(BF16)
        pieces.append(piece)
        value = value - piece.astype(F32)
    return pieces


def dot(a, b):
    return jnp.dot(a, b, preferred_element_type=F32)


def dot_t(a, b):
    return lax.dot_general(a, b, (((1,), (1,)), ((), ())), preferred_element_type=F32)


def kernel(
    sizes,
    e_hbm,
    mat_hbm,
    eps_ref,
    loss_ref,
    cell_ref,
    owner_ref,
    block_ref,
    x_hbm,
    u_hbm,
    d_hbm,
    s_hbm,
    e_out,
    h_out,
    x_out,
    e_ref,
    h_ref,
    mat_ref,
    keep_ref,
    gain_ref,
    hist_ref,
    field_ref,
    x_ref,
    base_ref,
    u_ref,
    d_ref,
    s_ref,
    send_buf,
    recv_buf,
    coef_send,
    coef_recv,
    volt_send,
    volt_recv,
    gather_buf,
    in_sem,
    out_sem,
    send_sem,
    recv_sem,
    coef_ssem,
    coef_rsem,
    volt_ssem,
    volt_rsem,
):
    nz = sizes[2]
    cap = x_ref.shape[0] // nz
    slots = x_ref.shape[0]
    me = [lax.axis_index(a) for a in AXES]

    def exists(offset):
        ok = None
        for at, off, size in zip(me, offset, sizes):
            if off:
                one = at + off >= 0 if off < 0 else at + off < size
                ok = one if ok is None else jnp.logical_and(ok, one)
        return ok

    def device(offset):
        return tuple(at + off for at, off in zip(me, offset))

    def peer(step):
        return lax.rem(me[2] + step, nz)

    loads = [
        pltpu.make_async_copy(src, dst, in_sem.at[n])
        for n, (src, dst) in enumerate(
            (
                (e_hbm, e_ref),
                (mat_hbm, mat_ref),
                (x_hbm, x_ref),
                (u_hbm, u_ref),
                (d_hbm, d_ref),
                (s_hbm, s_ref),
            )
        )
    ]
    for load in loads:
        load.start()
    recv_buf[...] = jnp.zeros(recv_buf.shape, F32)

    barrier = pltpu.get_barrier_semaphore()
    arrivals = jnp.int32(nz - 1)
    for offset, _, _ in MESSAGES:
        if offset[:2] == (0, 0):
            continue
        ok = exists(offset)
        arrivals = arrivals + ok.astype(jnp.int32)

        @pl.when(ok)
        def _(offset=offset):
            pl.semaphore_signal(barrier, inc=1, device_id=device(offset), device_id_type=MESH)

    for step in range(1, nz):
        pl.semaphore_signal(
            barrier, inc=1, device_id=(me[0], me[1], peer(step)), device_id_type=MESH
        )

    row = iota((8, 128), 0)
    lane = iota((8, 128), 1)
    planes = range(8)

    for load in loads[:2]:
        load.wait()
    mat = [mat_ref[i] for i in planes]
    keep = [jnp.zeros((8, 128), F32) for _ in planes]
    gain = [jnp.zeros((8, 128), F32) for _ in planes]
    for m in range(eps_ref.shape[0]):
        loss = jnp.full((8, 128), loss_ref[m], F32)
        eps = jnp.full((8, 128), eps_ref[m], F32)
        keep_m = (1.0 - loss) / (1.0 + loss)
        gain_m = 0.5 / (eps * (1.0 + loss))
        for i in planes:
            same = mat[i] == m
            keep[i] = jnp.where(same, keep_m, keep[i])
            gain[i] = jnp.where(same, gain_m, gain[i])
    for i in planes:
        keep_ref[i] = keep[i]
        gain_ref[i] = gain[i]

    def pack_y(c, j):
        tile = jnp.zeros((8, 128), F32)
        for i in planes:
            tile = jnp.where(row == i, full(e_ref[c, i, j : j + 1, :]), tile)
        return tile

    def pack_z(comps, k):
        tile = jnp.zeros((8, 128), F32)
        for c in comps:
            for i in planes:
                tile = jnp.where(lane == c * 8 + i, full(e_ref[c, i][:, k : k + 1]), tile)
        return tile

    def pack(par):
        y7 = [pack_y(c, 7) for c in range(3)]
        z127 = pack_z((0, 1, 2), 127)
        tiles = [e_ref[c, 7] for c in range(3)]
        tiles += [e_ref[1, 0], e_ref[2, 0]]
        tiles += y7
        tiles += [pack_y(0, 0), pack_y(2, 0)]
        tiles += [z127, pack_z((0, 1), 0)]
        tiles += [pltpu.roll(e_ref[0, 7], 7, 0), pltpu.roll(y7[1], 7, 0)]
        tiles += [pltpu.roll(e_ref[0, 7], 127, 1), pltpu.roll(y7[1], 127, 1)]
        tiles += [pltpu.roll(z127, 7, 0), pltpu.roll(z127, 7, 1)]
        for t, tile in enumerate(tiles):
            send_buf[par, t] = tile

    def message(m, par):
        offset, first, count = MESSAGES[m]
        return pltpu.make_async_remote_copy(
            src_ref=send_buf.at[par, pl.ds(first, count)],
            dst_ref=recv_buf.at[par, pl.ds(first, count)],
            send_sem=send_sem.at[par, m],
            recv_sem=recv_sem.at[par, m],
            device_id=device(offset),
            device_id_type=MESH,
        )

    def send_faces(par):
        for m, (offset, _, _) in enumerate(MESSAGES):

            @pl.when(exists(offset))
            def _(m=m):
                message(m, par).start()

    def wait_faces(par):
        for m, (offset, _, _) in enumerate(MESSAGES):

            @pl.when(exists(tuple(-o for o in offset)))
            def _(m=m):
                message(m, par).wait_recv()

        for m, (offset, _, _) in enumerate(MESSAGES):

            @pl.when(exists(offset))
            def _(m=m):
                message(m, par).wait_send()

    pack(0)

    ports = cell_ref.shape[0]
    owners = [owner_ref[q, 0] for q in range(ports)]
    srow = iota((slots, 128), 0)
    slane = iota((slots, 128), 1)
    slot_cell = jnp.full((slots, 128), -1, jnp.int32)
    lane_cell = jnp.full((8, 128), -1, jnp.int32)
    for q in range(ports):
        index = owners[q] * cap
        for r in range(q):
            index = index + jnp.where(owners[r] == owners[q], 1, 0)
        slot_cell = jnp.where(srow == index, cell_ref[q], slot_cell)
        lane_cell = jnp.where(lax.rem(lane, slots) == index, cell_ref[q], lane_cell)
    in_lane = jnp.logical_and(slot_cell >= 0, (slot_cell & 127) == slane)
    gather = jnp.where((slot_cell >> 7) == lax.rem(slane, 64), 1.0, 0.0).astype(BF16)
    in_row = jnp.broadcast_to((lane_cell >> 7)[0:1, :], (64, 128))
    scatter = jnp.where(in_row == iota((64, 128), 0), 1.0, 0.0).astype(BF16)

    for load in loads[2:]:
        load.wait()
    brow = iota((slots + 8, 128), 0)
    which = jnp.where(brow == slots + 1, 1, 0)
    for s in range(slots):
        which = jnp.where(brow == s, block_ref[s], which)
    first = jnp.concatenate([which, which], axis=1) == 0
    nodes = x_ref.shape[1]
    state = jnp.concatenate(
        [x_ref[...], d_ref[...], jnp.zeros((6, nodes), F32)], axis=0
    )
    sense = jnp.where(
        first,
        jnp.broadcast_to(s_ref[0:1, :], first.shape),
        jnp.broadcast_to(s_ref[1:2, :], first.shape),
    )
    halves = [split(u_ref[b], 2) for b in range(2)]
    drives = [state[slots : slots + 2]]
    readouts = [jnp.sum(state * sense, axis=1, keepdims=True)]
    for n in range(ITERS):
        hi, lo = split(state, 2)
        both = [
            dot_t(hi, high) + (dot_t(hi, low) + dot_t(lo, high)) for high, low in halves
        ]
        state = jnp.where(first, both[0], both[1])
        readouts.append(jnp.sum(state * sense, axis=1, keepdims=True))
        if n < ITERS - 1:
            drives.append(state[slots : slots + 2])
    base_ref[...] = state[:slots]
    is_first = first[:slots, :128]
    coefs = jnp.zeros((slots, 128), F32)
    for n in range(ITERS):
        coefs = jnp.where(slane == n, readouts[n + 1][:slots], coefs)
        kick = jnp.where(is_first, readouts[n][slots : slots + 1], readouts[n][slots + 1 : slots + 2])
        coefs = jnp.where(slane == ITERS + n, kick, coefs)
    for g in range(nz):
        coef_send[g] = coefs[g * cap : (g + 1) * cap]

    pl.semaphore_wait(barrier, arrivals)

    send_faces(0)

    def exchange(step, src, dst, ssem, rsem):
        there = peer(step)
        return pltpu.make_async_remote_copy(
            src_ref=src.at[there],
            dst_ref=dst.at[me[2]],
            send_sem=ssem.at[step],
            recv_sem=rsem.at[step],
            device_id=(me[0], me[1], there),
            device_id_type=MESH,
        )

    coef_copies = [
        exchange(step, coef_send, coef_recv, coef_ssem, coef_rsem) for step in range(1, nz)
    ]
    for copy in coef_copies:
        copy.start()
    coef_recv[me[2]] = coef_send[me[2]]

    low = [jnp.where(me[d] > 0, 1.0, 0.0).astype(F32) for d in range(3)]
    ghosts = None
    volts = []

    for n in range(ITERS):
        par = n % 2
        e_z = [e_ref[2, i] for i in planes]
        for i in planes:
            hist_ref[n, i] = e_z[i]
        stack = jnp.concatenate(e_z, axis=0)
        found = dot(gather, jnp.concatenate(split(stack, 2), axis=0))
        volts.append(
            jnp.sum(jnp.where(in_lane, found, 0.0), axis=1, keepdims=True)
        )
        if n == ITERS - 1:
            tile = jnp.zeros((slots, 128), F32)
            for k in range(ITERS):
                tile = jnp.where(slane == k, volts[k], tile)
            for g in range(nz):
                volt_send[g] = tile[g * cap : (g + 1) * cap]
            volt_copies = [
                exchange(step, volt_send, volt_recv, volt_ssem, volt_rsem)
                for step in range(1, nz)
            ]
            for copy in volt_copies:
                copy.start()
            volt_recv[me[2]] = volt_send[me[2]]

        wait_faces(par)

        def got(t, par=par):
            return recv_buf[par, t]

        ex_m, ey_m, ez_m = got(0), got(1), got(2)
        ex_k = jnp.where(lane == 127, got(14), pltpu.roll(ex_m, 127, 1))
        ex_j = jnp.where(row == 7, got(12), pltpu.roll(ex_m, 7, 0))
        hy_x = -0.5 * ((ex_k - ex_m) - (e_ref[2, 0] - ez_m))
        hz_x = -0.5 * ((e_ref[1, 0] - ey_m) - (ex_j - ex_m))
        fx_m, fy_m, fz_m = got(5), got(6), got(7)
        fx_0, fz_0 = send_buf[par, 8], send_buf[par, 9]
        fy_k = jnp.where(lane == 127, got(15), pltpu.roll(fy_m, 127, 1))
        fy_i = jnp.where(row == 7, got(13), pltpu.roll(fy_m, 7, 0))
        hx_y = -0.5 * ((fz_0 - fz_m) - (fy_k - fy_m))
        hz_y = -0.5 * ((fy_i - fy_m) - (fx_0 - fx_m))
        g_m, g_0 = got(10), send_buf[par, 11]
        gz_j = jnp.where(row == 7, got(16), pltpu.roll(g_m, 7, 0)) - g_m
        gz_i = jnp.where(lane == 23, got(17), pltpu.roll(g_m, 127, 1)) - g_m
        g_d = g_0 - g_m
        h_z = -0.5 * jnp.where(
            lane < 8, g_d - pltpu.roll(gz_i, 128 - 16, 1), pltpu.roll(gz_j, 128 - 8, 1) - g_d
        )
        new = [hy_x * low[0], hz_x * low[0], hx_y * low[1], hz_y * low[1], h_z * low[2]]
        ghosts = new if ghosts is None else [a + b for a, b in zip(ghosts, new)]
        hy_x, hz_x, hx_y, hz_y, h_z = ghosts

        zp = got(11)
        for i in planes:
            ex, ey, ez = e_ref[0, i], e_ref[1, i], e_ref[2, i]
            ex_j = jnp.where(row == 7, full(recv_buf[par, 8, i : i + 1, :]), pltpu.roll(ex, 7, 0))
            ez_j = jnp.where(row == 7, full(recv_buf[par, 9, i : i + 1, :]), pltpu.roll(ez, 7, 0))
            ex_k = jnp.where(lane == 127, full(zp[:, i : i + 1]), pltpu.roll(ex, 127, 1))
            ey_k = jnp.where(lane == 127, full(zp[:, 8 + i : 9 + i]), pltpu.roll(ey, 127, 1))
            ey_i = e_ref[1, i + 1] if i < 7 else got(3)
            ez_i = e_ref[2, i + 1] if i < 7 else got(4)
            hx = -0.5 * ((ez_j - ez) - (ey_k - ey))
            hy = -0.5 * ((ex_k - ex) - (ez_i - ez))
            hz = -0.5 * ((ey_i - ey) - (ex_j - ex))
            for c, value in enumerate((hx, hy, hz)):
                h_ref[c, i] = value if n == 0 else h_ref[c, i] + value

        if n == 0:
            for copy in coef_copies:
                copy.wait_recv()
            for copy in coef_copies:
                copy.wait_send()
            for g in range(nz):
                gather_buf[g * cap : (g + 1) * cap, :] = coef_recv[g]
            table = gather_buf[...]
            spread = jnp.concatenate(
                [
                    jnp.where(in_lane, jnp.broadcast_to(table[:, k : k + 1], (slots, 128)), 0.0)
                    for k in range(2 * ITERS)
                ],
                axis=1,
            )
            pieces = split(spread, 3) + [jnp.zeros(spread.shape, BF16)]
            field_ref[...] = dot(scatter, jnp.concatenate(pieces, axis=0))

        for i in planes:
            hx, hy, hz = h_ref[0, i], h_ref[1, i], h_ref[2, i]
            hx_j = jnp.where(row == 0, full(hx_y[i : i + 1, :]), pltpu.roll(hx, 1, 0))
            hz_j = jnp.where(row == 0, full(hz_y[i : i + 1, :]), pltpu.roll(hz, 1, 0))
            hy_k = jnp.where(lane == 0, full(h_z[:, i : i + 1]), pltpu.roll(hy, 1, 1))
            hx_k = jnp.where(lane == 0, full(h_z[:, 8 + i : 9 + i]), pltpu.roll(hx, 1, 1))
            hy_i = h_ref[1, i - 1] if i > 0 else hy_x
            hz_i = h_ref[2, i - 1] if i > 0 else hz_x
            rows = slice(8 * i, 8 * i + 8)
            current = field_ref[rows, 128 * n : 128 * (n + 1)]
            for k in range(n + 1):
                at = ITERS + n - k
                current = current + field_ref[rows, 128 * at : 128 * (at + 1)] * hist_ref[k, i]
            keep, gain = keep_ref[i], gain_ref[i]
            e_ref[0, i] = keep * e_ref[0, i] + gain * ((hz - hz_j) - (hy - hy_k))
            e_ref[1, i] = keep * e_ref[1, i] + gain * ((hx - hx_k) - (hz - hz_i))
            e_ref[2, i] = keep * e_ref[2, i] + gain * (((hy - hy_i) - (hx - hx_j)) - current)

        if n < ITERS - 1:
            pack(1 - par)
            send_faces(1 - par)

    stores = [
        pltpu.make_async_copy(e_ref, e_out, out_sem.at[0]),
        pltpu.make_async_copy(h_ref, h_out, out_sem.at[1]),
        pltpu.make_async_copy(base_ref, x_out, out_sem.at[2]),
    ]
    stores[0].start()
    stores[1].start()

    for copy in volt_copies:
        copy.wait_recv()
    for copy in volt_copies:
        copy.wait_send()
    for g in range(nz):
        gather_buf[g * cap : (g + 1) * cap, :] = volt_recv[g]
    table = gather_buf[...]
    final = base_ref[...]
    pick = first[:slots]
    for k in range(ITERS):
        drive = drives[ITERS - 1 - k]
        rows = jnp.where(
            pick,
            jnp.broadcast_to(drive[0:1], final.shape),
            jnp.broadcast_to(drive[1:2], final.shape),
        )
        final = final + rows * table[:, k : k + 1]
    base_ref[...] = final
    stores[2].start()
    for store in stores:
        store.wait()


def solution(mesh):
    sizes = tuple(mesh.shape[a] for a in AXES)

    def local(
        e_field,
        material,
        permittivity,
        loss,
        port_cell,
        port_owner,
        circuit_block,
        circuit_state,
        mna_update,
        mna_drive,
        mna_sense,
    ):
        slots, nodes = circuit_state.shape
        cap = slots // sizes[2]
        anywhere = pl.BlockSpec(memory_space=pl.ANY)
        scalars = pl.BlockSpec(memory_space=pltpu.SMEM)
        dma = pltpu.SemaphoreType.DMA
        return pl.pallas_call(
            functools.partial(kernel, sizes),
            out_shape=[
                jax.ShapeDtypeStruct(e_field.shape, F32),
                jax.ShapeDtypeStruct(e_field.shape, F32),
                jax.ShapeDtypeStruct(circuit_state.shape, F32),
            ],
            in_specs=[anywhere] * 2 + [scalars] * 5 + [anywhere] * 4,
            out_specs=[anywhere] * 3,
            scratch_shapes=[
                pltpu.VMEM(e_field.shape, F32),
                pltpu.VMEM(e_field.shape, F32),
                pltpu.VMEM(material.shape, jnp.int32),
                pltpu.VMEM(material.shape, F32),
                pltpu.VMEM(material.shape, F32),
                pltpu.VMEM((ITERS,) + material.shape, F32),
                pltpu.VMEM((64, 2 * ITERS * 128), F32),
                pltpu.VMEM(circuit_state.shape, F32),
                pltpu.VMEM(circuit_state.shape, F32),
                pltpu.VMEM(mna_update.shape, F32),
                pltpu.VMEM(mna_drive.shape, F32),
                pltpu.VMEM(mna_sense.shape, F32),
                pltpu.VMEM((2, TILES, 8, 128), F32),
                pltpu.VMEM((2, TILES, 8, 128), F32),
                pltpu.VMEM((sizes[2], cap, 128), F32),
                pltpu.VMEM((sizes[2], cap, 128), F32),
                pltpu.VMEM((sizes[2], cap, 128), F32),
                pltpu.VMEM((sizes[2], cap, 128), F32),
                pltpu.VMEM((slots, 128), F32),
                dma((6,)),
                dma((3,)),
                dma((2, len(MESSAGES))),
                dma((2, len(MESSAGES))),
                dma((sizes[2],)),
                dma((sizes[2],)),
                dma((sizes[2],)),
                dma((sizes[2],)),
            ],
            compiler_params=pltpu.CompilerParams(
                collective_id=0, has_side_effects=True, vmem_limit_bytes=32 * 1024 * 1024
            ),
        )(
            e_field,
            material,
            permittivity,
            loss,
            port_cell,
            port_owner,
            circuit_block,
            circuit_state,
            mna_update,
            mna_drive,
            mna_sense,
        )

    placed = (
        P(None, "gx", "gy", "gz"),
        P("gx", "gy", "gz"),
        P(),
        P(),
        P(("gx", "gy", "gz")),
        P(("gx", "gy", "gz"), None),
        P(("gx", "gy", "gz")),
        P(("gx", "gy", "gz"), None),
        P(("gx", "gy", "gz"), None, None),
        P(("gx", "gy", "gz"), None),
        P(("gx", "gy", "gz"), None),
    )
    return jax.shard_map(
        local,
        mesh=mesh,
        in_specs=placed,
        out_specs=(
            P(None, "gx", "gy", "gz"),
            P(None, "gx", "gy", "gz"),
            P(("gx", "gy", "gz"), None),
        ),
        check_vma=False,
    )
```

time: 275 us -> 60.9 us (0.22); the launches traced: 272 us -> 60.5 us
  starting transfers between devices: 114 us -> 0 us
  waiting for transfers between devices: 96.6 us -> 0 us
  Pallas kernels: 0 us -> 53.7 us
  blocking collectives: 21.7 us -> 0 us
  local copies, waits for them, and re-layouts: 22.2 us -> 6.13 us
  other arithmetic: 11.1 us -> 0 us
  matrix products: 4.8 us -> 0 us
    ppermute x24 -> x0, starting transfers between devices: 72.8 us -> none  [the longest x12 51.8 us: with_halo(): lax.ppermute(lax.slice_in_dim(block, block.shape[dim] - width, None, axis...]
    all_to_all x7 -> x0, waiting for transfers between devices: 55.7 us -> none  [the longest x4 34.7 us: local(): lax.all_to_all(outgoing, 'gz', split_axis=0, concat_axis=0, tiled=True)]
    pallas_call x0 -> x1, Pallas kernels: none -> 53.7 us  [local(): pl.pallas_call(functools.partial(kernel, sizes), out_shape=[jax.ShapeDtyp...]
    all_to_all x7 -> x0, starting transfers between devices: 41 us -> none  [the longest x4 30.6 us: local(): lax.all_to_all(outgoing, 'gz', split_axis=0, concat_axis=0, tiled=True)]
    ppermute x24 -> x0, waiting for transfers between devices: 40.9 us -> none  [the longest x12 40.9 us: with_halo(): lax.ppermute(lax.slice_in_dim(block, 0, width, axis=dim), axis, backward)]
    all_to_all x1 -> x0, blocking collectives: 21.7 us -> none  [local(): lax.all_to_all(current.reshape(groups, send_cap), 'gz', split_axis=0, con...]
    all_to_all x13 -> x0, local copies, waits for them, and re-layouts: 5.72 us -> none  [the longest x5 3.24 us: local(): lax.all_to_all(outgoing, 'gz', split_axis=0, concat_axis=0, tiled=True)]
    gather x8 -> x0, local copies, waits for them, and re-layouts: 5.36 us -> none  [the longest x4 2.74 us: local(): port_current = returned[owners, slot_index]]
  transfers between devices with their start and end apart: 31 -> 0, of which waited for: 15 -> 0; matrix products, arithmetic and copies ran while one was open for 11% -> 0% of each run, Pallas kernels for 0% -> 0%
where the time goes in v1:
time: 60.9 us; the launch traced here: 60.5 us
  Pallas kernels  53.7 us (88%)
  local copies, waits for them, and re-layouts  6.13 us (10%)
  between operations  0.73 us (1%)
    pallas_call x1, Pallas kernels, local(): pl.pallas_call(functools.partial(kernel, sizes), out_shape=[jax.ShapeDtyp...  53.7 us
    unnamed x24, local copies, waits for them, and re-layouts  6.13 us

profile of v1, /device:TPU:6, one launch (start us, length us, event | category | flops | bytes accessed | tf_op | source)
XLA Modules:
  0.0 60.5 jit_solution(9529235597278432887)
XLA Ops:
  0.6 0.0 copy-start.5
  0.6 0.0 copy-start.4
  0.7 0.0 copy-start.9
  0.7 0.0 copy-start.8
  0.7 0.0 copy-start.7
  0.7 0.0 copy-start.6
  0.7 0.8 %copy.14.owner_ref = s32[16,1]{1,0:T(8,128)S(1)} copy(s32[16,1]{0,1:T(1,128)} %param.16) | data formatting | bytes 128 | tf_op args[5]
  1.5 0.0 copy-done.5
  1.5 0.0 copy-done.4
  1.5 0.0 copy-done.9
  1.5 0.0 copy-done.8
  1.5 0.0 copy-done.7
  1.5 0.0 copy-done.6
  1.5 0.0 copy-start
  1.5 1.0 %copy-done = f32[2,256,256]{2,1,0:T(8,128)S(1)} copy-done((f32[2,256,256]{2,1,0:T(8,128)S(1)}, f32[2,256,256]{2,1,0:T(8,128)}, u32[]{:S(2)}) %copy-start) | copy-done | bytes 524312
  2.5 0.0 copy-start.1
  2.5 0.9 %copy-done.1 = f32[3,8,8,128]{3,2,1,0:T(8,128)S(1)} copy-done((f32[3,8,8,128]{3,2,1,0:T(8,128)S(1)}, f32[3,8,8,128]{3,2,1,0:T(8,128)}, u32[]{:S(2)}) %copy-start.1) | copy-done | bytes 98328
  3.4 0.0 copy-start.2
  3.4 0.8 %copy-done.2 = s32[8,8,128]{2,1,0:T(8,128)S(1)} copy-done((s32[8,8,128]{2,1,0:T(8,128)S(1)}, s32[8,8,128]{2,1,0:T(8,128)}, u32[]{:S(2)}) %copy-start.2) | copy-done | bytes 32792
  4.2 0.8 %copy-done.3 = f32[32,256]{1,0:T(8,128)S(1)} copy-done((f32[32,256]{1,0:T(8,128)S(1)}, f32[32,256]{1,0:T(8,128)}, u32[]{:S(2)}) %copy-start.3) | copy-done | bytes 32792
  5.0 53.7 %shard_map.130 = (f32[3,8,8,128]{3,2,1,0:T(8,128)S(1)}, f32[3,8,8,128]{3,2,1,0:T(8,128)S(1)}, f32[32,256]{1,0:T(8,128)S(1)}) custom-call(f32[3,8,8,128]{3,2,1,0:T(8,128)S(1)} %copy-done.1, s32[8,8,128]{2,1,0:T(8,128)S(1)} %copy-done.2, f32[16]{0:T(128)S(1)} %copy-done.6, f32[16]{0:T(128)S(1)} %copy-done.7, s32[16]{0:T(128)S(1)} %copy-done.8, ...), custom_call_target="tpu_custom_call" | custom-call | tf_op jit(solution)/shard_map/pallas_call | solution.py:476
  58.6 0.6 %copy.18 = f32[3,8,8,128]{3,2,1,0:T(8,128)} copy(f32[3,8,8,128]{3,2,1,0:T(8,128)S(1)} %get-tuple-element.6) | data formatting | bytes 196608
  59.3 0.6 %copy.19 = f32[3,8,8,128]{3,2,1,0:T(8,128)} copy(f32[3,8,8,128]{3,2,1,0:T(8,128)S(1)} %get-tuple-element.7) | data formatting | bytes 196608
  59.9 0.6 %copy.20 = f32[32,256]{1,0:T(8,128)} copy(f32[32,256]{1,0:T(8,128)S(1)} %get-tuple-element.8) | data formatting | bytes 65536
  (1 shorter events, 0.0 us)
Async XLA Ops:
  0.6 0.8 %copy-start.5 = (f32[2,256]{1,0:T(2,128)S(1)}, f32[2,256]{1,0:T(2,128)}, u32[]{:S(2)}) copy-start(f32[2,256]{1,0:T(2,128)} %s_hbm.1) | copy-start | bytes 6148
  0.6 0.8 %copy-start.4 = (f32[2,256]{1,0:T(2,128)S(1)}, f32[2,256]{1,0:T(2,128)}, u32[]{:S(2)}) copy-start(f32[2,256]{1,0:T(2,128)} %d_hbm.1) | copy-start | bytes 6148
  0.7 0.8 %copy-start.9 = (s32[32]{0:T(128)S(1)}, s32[32]{0:T(128)}, u32[]{:S(2)}) copy-start(s32[32]{0:T(128)} %block_ref.1) | copy-start | bytes 388
  0.7 0.8 %copy-start.8 = (s32[16]{0:T(128)S(1)}, s32[16]{0:T(128)}, u32[]{:S(2)}) copy-start(s32[16]{0:T(128)} %cell_ref.1) | copy-start | bytes 196
  0.7 0.8 %copy-start.7 = (f32[16]{0:T(128)S(1)}, f32[16]{0:T(128)}, u32[]{:S(2)}) copy-start(f32[16]{0:T(128)} %loss_ref.1) | copy-start | bytes 196
  0.7 0.8 %copy-start.6 = (f32[16]{0:T(128)S(1)}, f32[16]{0:T(128)}, u32[]{:S(2)}) copy-start(f32[16]{0:T(128)} %eps_ref.1) | copy-start | bytes 196
  1.5 1.0 %copy-start = (f32[2,256,256]{2,1,0:T(8,128)S(1)}, f32[2,256,256]{2,1,0:T(8,128)}, u32[]{:S(2)}) copy-start(f32[2,256,256]{2,1,0:T(8,128)} %u_hbm.1) | copy-start | bytes 1572868
  2.5 0.9 %copy-start.1 = (f32[3,8,8,128]{3,2,1,0:T(8,128)S(1)}, f32[3,8,8,128]{3,2,1,0:T(8,128)}, u32[]{:S(2)}) copy-start(f32[3,8,8,128]{3,2,1,0:T(8,128)} %e_hbm.1) | copy-start | bytes 294916
  3.4 0.8 %copy-start.2 = (s32[8,8,128]{2,1,0:T(8,128)S(1)}, s32[8,8,128]{2,1,0:T(8,128)}, u32[]{:S(2)}) copy-start(s32[8,8,128]{2,1,0:T(8,128)} %mat_hbm.1) | copy-start | bytes 98308
  4.2 0.8 %copy-start.3 = (f32[32,256]{1,0:T(8,128)S(1)}, f32[32,256]{1,0:T(8,128)}, u32[]{:S(2)}) copy-start(f32[32,256]{1,0:T(8,128)} %x_hbm.1) | copy-start | bytes 98308

commit v2 on v1

--- a/solution.py
+++ b/solution.py
@@ -14,18 +14,18 @@
 BF16 = jnp.bfloat16
 
 MESSAGES = (
+    ((1, 0, -1), 14, 1),
+    ((-1, 0, 1), 17, 1),
+    ((1, -1, 0), 12, 1),
+    ((-1, 1, 0), 13, 1),
     ((1, 0, 0), 0, 3),
     ((-1, 0, 0), 3, 2),
+    ((0, -1, 1), 16, 1),
+    ((0, 1, -1), 15, 1),
+    ((0, 0, 1), 10, 1),
+    ((0, 0, -1), 11, 1),
     ((0, 1, 0), 5, 3),
     ((0, -1, 0), 8, 2),
-    ((0, 0, 1), 10, 1),
-    ((0, 0, -1), 11, 1),
-    ((1, -1, 0), 12, 1),
-    ((-1, 1, 0), 13, 1),
-    ((1, 0, -1), 14, 1),
-    ((0, 1, -1), 15, 1),
-    ((0, -1, 1), 16, 1),
-    ((-1, 0, 1), 17, 1),
 )
 TILES = 18
 
@@ -59,27 +59,29 @@
     sizes,
     e_hbm,
     mat_hbm,
+    eps_hbm,
+    loss_hbm,
+    cell_hbm,
+    owner_hbm,
+    block_hbm,
+    x_hbm,
+    u_hbm,
+    d_hbm,
+    s_hbm,
+    e_ref,
+    h_ref,
+    base_ref,
     eps_ref,
     loss_ref,
     cell_ref,
     owner_ref,
     block_ref,
-    x_hbm,
-    u_hbm,
-    d_hbm,
-    s_hbm,
-    e_out,
-    h_out,
-    x_out,
-    e_ref,
-    h_ref,
     mat_ref,
     keep_ref,
     gain_ref,
     hist_ref,
     field_ref,
     x_ref,
-    base_ref,
     u_ref,
     d_ref,
     s_ref,
@@ -91,7 +93,6 @@
     volt_recv,
     gather_buf,
     in_sem,
-    out_sem,
     send_sem,
     recv_sem,
     coef_ssem,
@@ -124,15 +125,19 @@
             (
                 (e_hbm, e_ref),
                 (mat_hbm, mat_ref),
+                (eps_hbm, eps_ref),
+                (loss_hbm, loss_ref),
+                (cell_hbm, cell_ref),
+                (owner_hbm, owner_ref),
+                (block_hbm, block_ref),
+                (u_hbm, u_ref),
                 (x_hbm, x_ref),
-                (u_hbm, u_ref),
                 (d_hbm, d_ref),
                 (s_hbm, s_ref),
             )
         )
     ]
-    for load in loads:
-        load.start()
+
     recv_buf[...] = jnp.zeros(recv_buf.shape, F32)
 
     barrier = pltpu.get_barrier_semaphore()
@@ -152,11 +157,14 @@
             barrier, inc=1, device_id=(me[0], me[1], peer(step)), device_id_type=MESH
         )
 
+    for load in loads:
+        load.start()
+
     row = iota((8, 128), 0)
     lane = iota((8, 128), 1)
     planes = range(8)
 
-    for load in loads[:2]:
+    for load in loads[1:7]:
         load.wait()
     mat = [mat_ref[i] for i in planes]
     keep = [jnp.zeros((8, 128), F32) for _ in planes]
@@ -232,10 +240,11 @@
             def _(m=m):
                 message(m, par).wait_send()
 
+    loads[0].wait()
     pack(0)
 
     ports = cell_ref.shape[0]
-    owners = [owner_ref[q, 0] for q in range(ports)]
+    owners = [owner_ref[q] for q in range(ports)]
     srow = iota((slots, 128), 0)
     slane = iota((slots, 128), 1)
     slot_cell = jnp.full((slots, 128), -1, jnp.int32)
@@ -251,7 +260,7 @@
     in_row = jnp.broadcast_to((lane_cell >> 7)[0:1, :], (64, 128))
     scatter = jnp.where(in_row == iota((64, 128), 0), 1.0, 0.0).astype(BF16)
 
-    for load in loads[2:]:
+    for load in loads[7:]:
         load.wait()
     brow = iota((slots + 8, 128), 0)
     which = jnp.where(brow == slots + 1, 1, 0)
@@ -421,14 +430,6 @@
             pack(1 - par)
             send_faces(1 - par)
 
-    stores = [
-        pltpu.make_async_copy(e_ref, e_out, out_sem.at[0]),
-        pltpu.make_async_copy(h_ref, h_out, out_sem.at[1]),
-        pltpu.make_async_copy(base_ref, x_out, out_sem.at[2]),
-    ]
-    stores[0].start()
-    stores[1].start()
-
     for copy in volt_copies:
         copy.wait_recv()
     for copy in volt_copies:
@@ -447,9 +448,18 @@
         )
         final = final + rows * table[:, k : k + 1]
     base_ref[...] = final
-    stores[2].start()
-    for store in stores:
-        store.wait()
+
+
+def hand_out(*refs):
+    sources, results, sem = refs[:3], refs[3:6], refs[6]
+    copies = [
+        pltpu.make_async_copy(src, dst, sem.at[n])
+        for n, (src, dst) in enumerate(zip(sources, results))
+    ]
+    for copy in copies:
+        copy.start()
+    for copy in copies:
+        copy.wait()
 
 
 def solution(mesh):
@@ -470,27 +480,26 @@
     ):
         slots, nodes = circuit_state.shape
         cap = slots // sizes[2]
-        anywhere = pl.BlockSpec(memory_space=pl.ANY)
-        scalars = pl.BlockSpec(memory_space=pltpu.SMEM)
+        hbm = pl.BlockSpec(memory_space=pltpu.HBM)
         dma = pltpu.SemaphoreType.DMA
-        return pl.pallas_call(
+        vmem = pl.BlockSpec(memory_space=pltpu.VMEM)
+        shapes = (e_field.shape, e_field.shape, circuit_state.shape)
+        results = pl.pallas_call(
             functools.partial(kernel, sizes),
-            out_shape=[
-                jax.ShapeDtypeStruct(e_field.shape, F32),
-                jax.ShapeDtypeStruct(e_field.shape, F32),
-                jax.ShapeDtypeStruct(circuit_state.shape, F32),
-            ],
-            in_specs=[anywhere] * 2 + [scalars] * 5 + [anywhere] * 4,
-            out_specs=[anywhere] * 3,
+            out_shape=[pltpu.VMEM(shape, F32) for shape in shapes],
+            in_specs=[hbm] * 11,
+            out_specs=[vmem] * 3,
             scratch_shapes=[
-                pltpu.VMEM(e_field.shape, F32),
-                pltpu.VMEM(e_field.shape, F32),
+                pltpu.SMEM(permittivity.shape, F32),
+                pltpu.SMEM(loss.shape, F32),
+                pltpu.SMEM(port_cell.shape, jnp.int32),
+                pltpu.SMEM(port_cell.shape, jnp.int32),
+                pltpu.SMEM(circuit_block.shape, jnp.int32),
                 pltpu.VMEM(material.shape, jnp.int32),
                 pltpu.VMEM(material.shape, F32),
                 pltpu.VMEM(material.shape, F32),
                 pltpu.VMEM((ITERS,) + material.shape, F32),
                 pltpu.VMEM((64, 2 * ITERS * 128), F32),
-                pltpu.VMEM(circuit_state.shape, F32),
                 pltpu.VMEM(circuit_state.shape, F32),
                 pltpu.VMEM(mna_update.shape, F32),
                 pltpu.VMEM(mna_drive.shape, F32),
@@ -502,8 +511,7 @@
                 pltpu.VMEM((sizes[2], cap, 128), F32),
                 pltpu.VMEM((sizes[2], cap, 128), F32),
                 pltpu.VMEM((slots, 128), F32),
-                dma((6,)),
-                dma((3,)),
+                dma((11,)),
                 dma((2, len(MESSAGES))),
                 dma((2, len(MESSAGES))),
                 dma((sizes[2],)),
@@ -515,18 +523,30 @@
                 collective_id=0, has_side_effects=True, vmem_limit_bytes=32 * 1024 * 1024
             ),
         )(
-            e_field,
-            material,
-            permittivity,
-            loss,
-            port_cell,
-            port_owner,
-            circuit_block,
-            circuit_state,
-            mna_update,
-            mna_drive,
-            mna_sense,
-        )
+            *(
+                pltpu.with_memory_space_constraint(array, pltpu.HBM)
+                for array in (
+                    e_field,
+                    material,
+                    permittivity,
+                    loss,
+                    port_cell,
+                    port_owner.reshape(-1),
+                    circuit_block,
+                    circuit_state,
+                    mna_update,
+                    mna_drive,
+                    mna_sense,
+                )
+            )
+        )
+        return pl.pallas_call(
+            hand_out,
+            out_shape=[jax.ShapeDtypeStruct(shape, F32) for shape in shapes],
+            in_specs=[vmem] * 3,
+            out_specs=[hbm] * 3,
+            scratch_shapes=[dma((3,))],
+        )(*(pltpu.with_memory_space_constraint(r, pltpu.VMEM) for r in results))
 
     placed = (
         P(None, "gx", "gy", "gz"),

time: 60.9 us -> 54.1 us (0.89)
  local copies, waits for them, and re-layouts: 6.13 us -> 0 us
    unnamed x24 -> x0, local copies, waits for them, and re-layouts: 6.13 us -> none
    pallas_call x1 -> x2, Pallas kernels: 53.7 us -> 53.3 us  [the longest x1 52.6 us: local(): pl.pallas_call(functools.partial(kernel, sizes), out_shape=[pltpu.VMEM(sh...]
where the time goes in v2:
time: 54.1 us; the launch traced here: 53.9 us
  Pallas kernels  53.3 us (99%)
  between operations  0.64 us (1%)
    pallas_call x1, Pallas kernels, local(): pl.pallas_call(functools.partial(kernel, sizes), out_shape=[pltpu.VMEM(sh...  52.6 us

profile of v2, /device:TPU:6, one launch (start us, length us, event | category | flops | bytes accessed | tf_op | source)
XLA Modules:
  0.0 53.9 jit_solution(6127972910921910446)
XLA Ops:
  0.6 52.6 %shard_map.130 = (f32[3,8,8,128]{3,2,1,0:T(8,128)S(1)}, f32[3,8,8,128]{3,2,1,0:T(8,128)S(1)}, f32[32,256]{1,0:T(8,128)S(1)}) custom-call(f32[3,8,8,128]{3,2,1,0:T(8,128)} %e_hbm.1, s32[8,8,128]{2,1,0:T(8,128)} %mat_hbm.1, f32[16]{0:T(128)} %eps_hbm.1, f32[16]{0:T(128)} %loss_hbm.1, s32[16]{0:T(128)} %cell_hbm.1, s32[16]{0:T(128)} %bitcast.1, s32[32]{0:T(128)} %block_hbm.1, ...), custom_call_target="tpu_custom_call" | custom-call | tf_op jit(solution)/shard_map/pallas_call | solution.py:487
  53.2 0.7 %shard_map.131 = (f32[3,8,8,128]{3,2,1,0:T(8,128)}, f32[3,8,8,128]{3,2,1,0:T(8,128)}, f32[32,256]{1,0:T(8,128)}) custom-call(f32[3,8,8,128]{3,2,1,0:T(8,128)S(1)} %get-tuple-element.6.refs_0_, f32[3,8,8,128]{3,2,1,0:T(8,128)S(1)} %get-tuple-element.7.refs_1_, f32[32,256]{1,0:T(8,128)S(1)} %get-tuple-element.8.refs_2_), custom_call_target="tpu_custom_call" | custom-call | tf_op jit(solution)/shard_map/pallas_call | solution.py:543

commit v3 on v2

--- a/solution.py
+++ b/solution.py
@@ -14,21 +14,23 @@
 BF16 = jnp.bfloat16
 
 MESSAGES = (
-    ((1, 0, -1), 14, 1),
-    ((-1, 0, 1), 17, 1),
-    ((1, -1, 0), 12, 1),
-    ((-1, 1, 0), 13, 1),
-    ((1, 0, 0), 0, 3),
-    ((-1, 0, 0), 3, 2),
-    ((0, -1, 1), 16, 1),
-    ((0, 1, -1), 15, 1),
-    ((0, 0, 1), 10, 1),
-    ((0, 0, -1), 11, 1),
-    ((0, 1, 0), 5, 3),
-    ((0, -1, 0), 8, 2),
+    ((1, 0, -1), 0, 1, 1),
+    ((-1, 0, 1), 2, 1, 1),
+    ((1, 0, 0), 4, 3, 1),
+    ((-1, 0, 0), 8, 2, 1),
+    ((1, -1, 0), 11, 1, 1),
+    ((-1, 1, 0), 13, 1, 0),
+    ((0, -1, 1), 14, 1, 0),
+    ((0, 1, -1), 15, 1, 0),
+    ((0, 0, 1), 16, 1, 0),
+    ((0, 0, -1), 17, 1, 0),
+    ((0, 1, 0), 18, 3, 0),
+    ((0, -1, 0), 21, 2, 0),
 )
-TILES = 18
-
+TILES = 23
+LATE = (0, 1)
+FAR = range(6)
+NEAR = range(6, 12)
 
 def iota(shape, dim):
     return lax.broadcasted_iota(jnp.int32, shape, dim)
@@ -142,7 +144,7 @@
 
     barrier = pltpu.get_barrier_semaphore()
     arrivals = jnp.int32(nz - 1)
-    for offset, _, _ in MESSAGES:
+    for offset, _, _, _ in MESSAGES:
         if offset[:2] == (0, 0):
             continue
         ok = exists(offset)
@@ -195,53 +197,74 @@
                 tile = jnp.where(lane == c * 8 + i, full(e_ref[c, i][:, k : k + 1]), tile)
         return tile
 
-    def pack(par):
+    def pack_far(n):
+        e_x7, e_z0 = e_ref[0, 7], e_ref[2, 0]
+        tiles = {
+            0: pltpu.roll(e_x7, 127, 1),
+            2: pltpu.roll(e_z0, 24, 1),
+            4: e_x7,
+            5: e_ref[1, 7],
+            6: e_ref[2, 7],
+            8: e_ref[1, 0],
+            9: e_z0,
+            11: pltpu.roll(e_x7, 7, 0),
+            13: e_ref[1, 0],
+        }
+        for t, tile in tiles.items():
+            send_buf[n, t] = tile
+
+    def pack_gains():
+        send_buf[0, 1] = pltpu.roll(gain[7], 127, 1)
+        send_buf[0, 3] = pltpu.roll(gain[0], 24, 1)
+        send_buf[0, 7] = gain[7]
+        send_buf[0, 10] = gain[0]
+        send_buf[0, 12] = pltpu.roll(gain[7], 7, 0)
+
+    def pack_near(n):
         y7 = [pack_y(c, 7) for c in range(3)]
         z127 = pack_z((0, 1, 2), 127)
-        tiles = [e_ref[c, 7] for c in range(3)]
-        tiles += [e_ref[1, 0], e_ref[2, 0]]
-        tiles += y7
-        tiles += [pack_y(0, 0), pack_y(2, 0)]
-        tiles += [z127, pack_z((0, 1), 0)]
-        tiles += [pltpu.roll(e_ref[0, 7], 7, 0), pltpu.roll(y7[1], 7, 0)]
-        tiles += [pltpu.roll(e_ref[0, 7], 127, 1), pltpu.roll(y7[1], 127, 1)]
-        tiles += [pltpu.roll(z127, 7, 0), pltpu.roll(z127, 7, 1)]
+        tiles = [pltpu.roll(z127, 7, 0), pltpu.roll(y7[1], 127, 1), z127, pack_z((0, 1), 0)]
+        tiles += y7 + [pack_y(0, 0), pack_y(2, 0)]
         for t, tile in enumerate(tiles):
-            send_buf[par, t] = tile
-
-    def message(m, par):
-        offset, first, count = MESSAGES[m]
+            send_buf[n, 14 + t] = tile
+
+    def message(m, n):
+        offset, first, count, more = MESSAGES[m]
+        tiles = pl.ds(first, count + (more if n == 0 else 0))
         return pltpu.make_async_remote_copy(
-            src_ref=send_buf.at[par, pl.ds(first, count)],
-            dst_ref=recv_buf.at[par, pl.ds(first, count)],
-            send_sem=send_sem.at[par, m],
-            recv_sem=recv_sem.at[par, m],
+            src_ref=send_buf.at[n, tiles],
+            dst_ref=recv_buf.at[n, tiles],
+            send_sem=send_sem.at[n, m],
+            recv_sem=recv_sem.at[n, m],
             device_id=device(offset),
             device_id_type=MESH,
         )
 
-    def send_faces(par):
-        for m, (offset, _, _) in enumerate(MESSAGES):
-
-            @pl.when(exists(offset))
+    def send(which, n):
+        for m in which:
+
+            @pl.when(exists(MESSAGES[m][0]))
             def _(m=m):
-                message(m, par).start()
-
-    def wait_faces(par):
-        for m, (offset, _, _) in enumerate(MESSAGES):
-
-            @pl.when(exists(tuple(-o for o in offset)))
+                message(m, n).start()
+
+    def wait_recv(which, n):
+        for m in which:
+
+            @pl.when(exists(tuple(-o for o in MESSAGES[m][0])))
             def _(m=m):
-                message(m, par).wait_recv()
-
-        for m, (offset, _, _) in enumerate(MESSAGES):
-
-            @pl.when(exists(offset))
+                message(m, n).wait_recv()
+
+    def wait_send(n):
+        for m in range(len(MESSAGES)):
+
+            @pl.when(exists(MESSAGES[m][0]))
             def _(m=m):
-                message(m, par).wait_send()
+                message(m, n).wait_send()
 
     loads[0].wait()
-    pack(0)
+    pack_far(0)
+    pack_gains()
+    pack_near(0)
 
     ports = cell_ref.shape[0]
     owners = [owner_ref[q] for q in range(ports)]
@@ -300,7 +323,8 @@
 
     pl.semaphore_wait(barrier, arrivals)
 
-    send_faces(0)
+    send(FAR, 0)
+    send(NEAR, 0)
 
     def exchange(step, src, dst, ssem, rsem):
         there = peer(step)
@@ -322,10 +346,13 @@
 
     low = [jnp.where(me[d] > 0, 1.0, 0.0).astype(F32) for d in range(3)]
     ghosts = None
+    owed = None
     volts = []
 
+    def lacking(where, tile, value):
+        return jnp.where(where, 0.5 * recv_buf[0, tile], 0.0) * value
+
     for n in range(ITERS):
-        par = n % 2
         e_z = [e_ref[2, i] for i in planes]
         for i in planes:
             hist_ref[n, i] = e_z[i]
@@ -348,25 +375,29 @@
                 copy.start()
             volt_recv[me[2]] = volt_send[me[2]]
 
-        wait_faces(par)
-
-        def got(t, par=par):
-            return recv_buf[par, t]
-
-        ex_m, ey_m, ez_m = got(0), got(1), got(2)
-        ex_k = jnp.where(lane == 127, got(14), pltpu.roll(ex_m, 127, 1))
-        ex_j = jnp.where(row == 7, got(12), pltpu.roll(ex_m, 7, 0))
+        wait_recv([m for m in range(len(MESSAGES)) if m not in LATE], n)
+
+        def got(t, n=n):
+            return recv_buf[n, t]
+
+        ex_m, ey_m, ez_m = got(4), got(5), got(6)
+        ey_p, ez_p = got(8), got(9)
+        ex_edge = got(11)
+        if n > 0:
+            ex_m, ez_p, ex_edge = ex_m + owed[0], ez_p + owed[1], ex_edge + owed[2]
+        ex_k = jnp.where(lane == 127, 0.0, pltpu.roll(ex_m, 127, 1))
+        ex_j = jnp.where(row == 7, ex_edge, pltpu.roll(ex_m, 7, 0))
         hy_x = -0.5 * ((ex_k - ex_m) - (e_ref[2, 0] - ez_m))
         hz_x = -0.5 * ((e_ref[1, 0] - ey_m) - (ex_j - ex_m))
-        fx_m, fy_m, fz_m = got(5), got(6), got(7)
-        fx_0, fz_0 = send_buf[par, 8], send_buf[par, 9]
+        fx_m, fy_m, fz_m = got(18), got(19), got(20)
+        fx_0, fz_0 = send_buf[n, 21], send_buf[n, 22]
         fy_k = jnp.where(lane == 127, got(15), pltpu.roll(fy_m, 127, 1))
         fy_i = jnp.where(row == 7, got(13), pltpu.roll(fy_m, 7, 0))
         hx_y = -0.5 * ((fz_0 - fz_m) - (fy_k - fy_m))
         hz_y = -0.5 * ((fy_i - fy_m) - (fx_0 - fx_m))
-        g_m, g_0 = got(10), send_buf[par, 11]
-        gz_j = jnp.where(row == 7, got(16), pltpu.roll(g_m, 7, 0)) - g_m
-        gz_i = jnp.where(lane == 23, got(17), pltpu.roll(g_m, 127, 1)) - g_m
+        g_m, g_0, g_edge = got(16), send_buf[n, 17], got(14)
+        gz_j = jnp.where(row == 7, g_edge, pltpu.roll(g_m, 7, 0)) - g_m
+        gz_i = jnp.where(lane == 23, 0.0, pltpu.roll(g_m, 127, 1)) - g_m
         g_d = g_0 - g_m
         h_z = -0.5 * jnp.where(
             lane < 8, g_d - pltpu.roll(gz_i, 128 - 16, 1), pltpu.roll(gz_j, 128 - 8, 1) - g_d
@@ -375,15 +406,25 @@
         ghosts = new if ghosts is None else [a + b for a, b in zip(ghosts, new)]
         hy_x, hz_x, hx_y, hz_y, h_z = ghosts
 
-        zp = got(11)
+        zp = got(17)
+        was_owed = owed
+        if n < ITERS - 1:
+            owed = [
+                lacking(lane == 0, 7, pltpu.roll(g_m, 112, 1)),
+                lacking(lane == 127, 10, pltpu.roll(zp, 120, 1)),
+                lacking(jnp.logical_and(lane == 0, row == 7), 12, pltpu.roll(g_edge, 112, 1)),
+                e_ref[2, 0],
+                pltpu.roll(e_ref[0, 7], 23, 1),
+            ]
+
         for i in planes:
             ex, ey, ez = e_ref[0, i], e_ref[1, i], e_ref[2, i]
-            ex_j = jnp.where(row == 7, full(recv_buf[par, 8, i : i + 1, :]), pltpu.roll(ex, 7, 0))
-            ez_j = jnp.where(row == 7, full(recv_buf[par, 9, i : i + 1, :]), pltpu.roll(ez, 7, 0))
+            ex_j = jnp.where(row == 7, full(recv_buf[n, 21, i : i + 1, :]), pltpu.roll(ex, 7, 0))
+            ez_j = jnp.where(row == 7, full(recv_buf[n, 22, i : i + 1, :]), pltpu.roll(ez, 7, 0))
             ex_k = jnp.where(lane == 127, full(zp[:, i : i + 1]), pltpu.roll(ex, 127, 1))
             ey_k = jnp.where(lane == 127, full(zp[:, 8 + i : 9 + i]), pltpu.roll(ey, 127, 1))
-            ey_i = e_ref[1, i + 1] if i < 7 else got(3)
-            ez_i = e_ref[2, i + 1] if i < 7 else got(4)
+            ey_i = e_ref[1, i + 1] if i < 7 else ey_p
+            ez_i = e_ref[2, i + 1] if i < 7 else ez_p
             hx = -0.5 * ((ez_j - ez) - (ey_k - ey))
             hy = -0.5 * ((ex_k - ex) - (ez_i - ez))
             hz = -0.5 * ((ey_i - ey) - (ex_j - ex))
@@ -393,8 +434,6 @@
         if n == 0:
             for copy in coef_copies:
                 copy.wait_recv()
-            for copy in coef_copies:
-                copy.wait_send()
             for g in range(nz):
                 gather_buf[g * cap : (g + 1) * cap, :] = coef_recv[g]
             table = gather_buf[...]
@@ -427,13 +466,27 @@
             e_ref[2, i] = keep * e_ref[2, i] + gain * (((hy - hy_i) - (hx - hx_j)) - current)
 
         if n < ITERS - 1:
-            pack(1 - par)
-            send_faces(1 - par)
+            pack_far(n + 1)
+            send(FAR, n + 1)
+
+        wait_recv(LATE, n)
+        x_edge, z_edge = got(0), got(2)
+        if n > 0:
+            x_edge = x_edge + lacking(lane == 127, 1, was_owed[3])
+            z_edge = z_edge + lacking(lane == 23, 3, was_owed[4])
+        x_edge = jnp.where(lane == 127, 0.5 * low[0] * x_edge, 0.0)
+        z_edge = jnp.where(lane == 23, 0.5 * low[2] * z_edge, 0.0)
+        ghosts[0] = ghosts[0] - x_edge
+        ghosts[4] = ghosts[4] + pltpu.roll(z_edge, 112, 1)
+        e_ref[2, 0] = e_ref[2, 0] + gain_ref[0] * x_edge
+        e_ref[0, 7] = e_ref[0, 7] + gain_ref[7] * pltpu.roll(z_edge, 105, 1)
+
+        if n < ITERS - 1:
+            pack_near(n + 1)
+            send(NEAR, n + 1)
 
     for copy in volt_copies:
         copy.wait_recv()
-    for copy in volt_copies:
-        copy.wait_send()
     for g in range(nz):
         gather_buf[g * cap : (g + 1) * cap, :] = volt_recv[g]
     table = gather_buf[...]
@@ -448,6 +501,10 @@
         )
         final = final + rows * table[:, k : k + 1]
     base_ref[...] = final
+    for copy in coef_copies + volt_copies:
+        copy.wait_send()
+    for n in range(ITERS):
+        wait_send(n)
 
 
 def hand_out(*refs):
@@ -504,16 +561,16 @@
                 pltpu.VMEM(mna_update.shape, F32),
                 pltpu.VMEM(mna_drive.shape, F32),
                 pltpu.VMEM(mna_sense.shape, F32),
-                pltpu.VMEM((2, TILES, 8, 128), F32),
-                pltpu.VMEM((2, TILES, 8, 128), F32),
+                pltpu.VMEM((ITERS, TILES, 8, 128), F32),
+                pltpu.VMEM((ITERS, TILES, 8, 128), F32),
                 pltpu.VMEM((sizes[2], cap, 128), F32),
                 pltpu.VMEM((sizes[2], cap, 128), F32),
                 pltpu.VMEM((sizes[2], cap, 128), F32),
                 pltpu.VMEM((sizes[2], cap, 128), F32),
                 pltpu.VMEM((slots, 128), F32),
                 dma((11,)),
-                dma((2, len(MESSAGES))),
-                dma((2, len(MESSAGES))),
+                dma((ITERS, len(MESSAGES))),
+                dma((ITERS, len(MESSAGES))),
                 dma((sizes[2],)),
                 dma((sizes[2],)),
                 dma((sizes[2],)),

time: 54.1 us -> 52.2 us (0.965)
  Pallas kernels: 53.3 us -> 51.4 us
    pallas_call x1, Pallas kernels: 52.6 us -> 50.7 us  [local(): pl.pallas_call(functools.partial(kernel, sizes), out_shape=[pltpu.VMEM(sh...]
where the time goes in v3:
time: 52.2 us; the launch traced here: 52.1 us
  Pallas kernels  51.4 us (98%)
  between operations  0.64 us (1%)
    pallas_call x1, Pallas kernels, local(): pl.pallas_call(functools.partial(kernel, sizes), out_shape=[pltpu.VMEM(sh...  50.7 us

profile of v3, /device:TPU:6, one launch (start us, length us, event | category | flops | bytes accessed | tf_op | source)
XLA Modules:
  0.0 52.1 jit_solution(4166793591147954820)
XLA Ops:
  0.6 50.7 %shard_map.130 = (f32[3,8,8,128]{3,2,1,0:T(8,128)S(1)}, f32[3,8,8,128]{3,2,1,0:T(8,128)S(1)}, f32[32,256]{1,0:T(8,128)S(1)}) custom-call(f32[3,8,8,128]{3,2,1,0:T(8,128)} %e_hbm.1, s32[8,8,128]{2,1,0:T(8,128)} %mat_hbm.1, f32[16]{0:T(128)} %eps_hbm.1, f32[16]{0:T(128)} %loss_hbm.1, s32[16]{0:T(128)} %cell_hbm.1, s32[16]{0:T(128)} %bitcast.1, s32[32]{0:T(128)} %block_hbm.1, ...), custom_call_target="tpu_custom_call" | custom-call | tf_op jit(solution)/shard_map/pallas_call | solution.py:544
  51.4 0.7 %shard_map.131 = (f32[3,8,8,128]{3,2,1,0:T(8,128)}, f32[3,8,8,128]{3,2,1,0:T(8,128)}, f32[32,256]{1,0:T(8,128)}) custom-call(f32[3,8,8,128]{3,2,1,0:T(8,128)S(1)} %get-tuple-element.6.refs_0_, f32[3,8,8,128]{3,2,1,0:T(8,128)S(1)} %get-tuple-element.7.refs_1_, f32[32,256]{1,0:T(8,128)S(1)} %get-tuple-element.8.refs_2_), custom_call_target="tpu_custom_call" | custom-call | tf_op jit(solution)/shard_map/pallas_call | solution.py:600

commit v4 on v3

--- a/solution.py
+++ b/solution.py
@@ -101,15 +101,17 @@
     coef_rsem,
     volt_ssem,
     volt_rsem,
+    peers_sem,
+    faces_sem,
 ):
     nz = sizes[2]
     cap = x_ref.shape[0] // nz
     slots = x_ref.shape[0]
     me = [lax.axis_index(a) for a in AXES]
 
-    def exists(offset):
+    def exists(offset, place=me):
         ok = None
-        for at, off, size in zip(me, offset, sizes):
+        for at, off, size in zip(place, offset, sizes):
             if off:
                 one = at + off >= 0 if off < 0 else at + off < size
                 ok = one if ok is None else jnp.logical_and(ok, one)
@@ -120,6 +122,8 @@
 
     def peer(step):
         return lax.rem(me[2] + step, nz)
+
+    others = sorted(range(1, nz), key=lambda step: -min(step, nz - step))
 
     loads = [
         pltpu.make_async_copy(src, dst, in_sem.at[n])
@@ -143,21 +147,35 @@
     recv_buf[...] = jnp.zeros(recv_buf.shape, F32)
 
     barrier = pltpu.get_barrier_semaphore()
-    arrivals = jnp.int32(nz - 1)
+    odd = lax.rem(me[1], 2)
+    is_even, is_odd = odd == 0, odd == 1
+    sibling = (me[0], me[1] + 1 - 2 * odd, me[2])
+    neighbours = jnp.int32(-1)
     for offset, _, _, _ in MESSAGES:
-        if offset[:2] == (0, 0):
-            continue
         ok = exists(offset)
-        arrivals = arrivals + ok.astype(jnp.int32)
+        neighbours = neighbours + ok.astype(jnp.int32)
+        neighbours = neighbours + exists(offset, (me[0], me[1] + 1, me[2])).astype(jnp.int32)
+        if offset == (0, 1, 0):
+            ok = jnp.logical_and(ok, is_odd)
 
         @pl.when(ok)
         def _(offset=offset):
-            pl.semaphore_signal(barrier, inc=1, device_id=device(offset), device_id_type=MESH)
-
-    for step in range(1, nz):
+            there = device(offset)
+            pl.semaphore_signal(
+                barrier,
+                inc=1,
+                device_id=(there[0], there[1] - lax.rem(there[1], 2), there[2]),
+                device_id_type=MESH,
+            )
+
+    for step in others:
         pl.semaphore_signal(
-            barrier, inc=1, device_id=(me[0], me[1], peer(step)), device_id_type=MESH
+            barrier, inc=1, device_id=(me[0], me[1] + 1 - odd, peer(step)), device_id_type=MESH
         )
+
+    @pl.when(is_even)
+    def _():
+        pl.semaphore_signal(barrier, inc=1, device_id=sibling, device_id_type=MESH)
 
     for load in loads:
         load.start()
@@ -321,11 +339,6 @@
     for g in range(nz):
         coef_send[g] = coefs[g * cap : (g + 1) * cap]
 
-    pl.semaphore_wait(barrier, arrivals)
-
-    send(FAR, 0)
-    send(NEAR, 0)
-
     def exchange(step, src, dst, ssem, rsem):
         there = peer(step)
         return pltpu.make_async_remote_copy(
@@ -338,11 +351,40 @@
         )
 
     coef_copies = [
-        exchange(step, coef_send, coef_recv, coef_ssem, coef_rsem) for step in range(1, nz)
+        exchange(step, coef_send, coef_recv, coef_ssem, coef_rsem) for step in others
     ]
-    for copy in coef_copies:
-        copy.start()
     coef_recv[me[2]] = coef_send[me[2]]
+
+    def start_circuits():
+        @pl.when(is_odd)
+        def _():
+            pl.semaphore_wait(barrier, 2 * (nz - 1) + 1)
+            pl.semaphore_signal(peers_sem, inc=1, device_id=sibling, device_id_type=MESH)
+
+        @pl.when(is_even)
+        def _():
+            pl.semaphore_wait(peers_sem, 1)
+
+        for copy in coef_copies:
+            copy.start()
+
+    def start_faces():
+        @pl.when(is_even)
+        def _():
+            pl.semaphore_wait(barrier, neighbours)
+            pl.semaphore_signal(faces_sem, inc=1, device_id=sibling, device_id_type=MESH)
+
+        @pl.when(is_odd)
+        def _():
+            pl.semaphore_wait(faces_sem, 1)
+
+        send(FAR, 0)
+        send(NEAR, 0)
+
+    last = me[2] >= nz - 2
+    pl.when(last)(start_circuits)
+    start_faces()
+    pl.when(jnp.logical_not(last))(start_circuits)
 
     low = [jnp.where(me[d] > 0, 1.0, 0.0).astype(F32) for d in range(3)]
     ghosts = None
@@ -352,122 +394,147 @@
     def lacking(where, tile, value):
         return jnp.where(where, 0.5 * recv_buf[0, tile], 0.0) * value
 
-    for n in range(ITERS):
+    def voltages(n):
         e_z = [e_ref[2, i] for i in planes]
         for i in planes:
             hist_ref[n, i] = e_z[i]
         stack = jnp.concatenate(e_z, axis=0)
         found = dot(gather, jnp.concatenate(split(stack, 2), axis=0))
-        volts.append(
-            jnp.sum(jnp.where(in_lane, found, 0.0), axis=1, keepdims=True)
+        volts.append(jnp.sum(jnp.where(in_lane, found, 0.0), axis=1, keepdims=True))
+
+    def send_voltages():
+        tile = jnp.zeros((slots, 128), F32)
+        for k in range(ITERS):
+            tile = jnp.where(slane == k, volts[k], tile)
+        for g in range(nz):
+            volt_send[g] = tile[g * cap : (g + 1) * cap]
+        copies = [exchange(step, volt_send, volt_recv, volt_ssem, volt_rsem) for step in others]
+        for copy in copies:
+            copy.start()
+        volt_recv[me[2]] = volt_send[me[2]]
+        return copies
+
+    def fields(table, ks):
+        spread = jnp.concatenate(
+            [
+                jnp.where(in_lane, jnp.broadcast_to(table[:, k : k + 1], (slots, 128)), 0.0)
+                for k in ks
+            ],
+            axis=1,
         )
-        if n == ITERS - 1:
-            tile = jnp.zeros((slots, 128), F32)
-            for k in range(ITERS):
-                tile = jnp.where(slane == k, volts[k], tile)
-            for g in range(nz):
-                volt_send[g] = tile[g * cap : (g + 1) * cap]
-            volt_copies = [
-                exchange(step, volt_send, volt_recv, volt_ssem, volt_rsem)
-                for step in range(1, nz)
-            ]
-            for copy in volt_copies:
-                copy.start()
-            volt_recv[me[2]] = volt_send[me[2]]
-
-        wait_recv([m for m in range(len(MESSAGES)) if m not in LATE], n)
+        pieces = split(spread, 3) + [jnp.zeros(spread.shape, BF16)]
+        found = dot(scatter, jnp.concatenate(pieces, axis=0))
+        for at, k in enumerate(ks):
+            field_ref[:, 128 * k : 128 * (k + 1)] = found[:, 128 * at : 128 * (at + 1)]
+
+    voltages(0)
+    for n in range(ITERS):
+        if n == ITERS - 1 and n == 0:
+            volt_copies = send_voltages()
 
         def got(t, n=n):
             return recv_buf[n, t]
 
-        ex_m, ey_m, ez_m = got(4), got(5), got(6)
-        ey_p, ez_p = got(8), got(9)
-        ex_edge = got(11)
-        if n > 0:
-            ex_m, ez_p, ex_edge = ex_m + owed[0], ez_p + owed[1], ex_edge + owed[2]
-        ex_k = jnp.where(lane == 127, 0.0, pltpu.roll(ex_m, 127, 1))
-        ex_j = jnp.where(row == 7, ex_edge, pltpu.roll(ex_m, 7, 0))
-        hy_x = -0.5 * ((ex_k - ex_m) - (e_ref[2, 0] - ez_m))
-        hz_x = -0.5 * ((e_ref[1, 0] - ey_m) - (ex_j - ex_m))
+        wait_recv(NEAR, n)
+
         fx_m, fy_m, fz_m = got(18), got(19), got(20)
         fx_0, fz_0 = send_buf[n, 21], send_buf[n, 22]
         fy_k = jnp.where(lane == 127, got(15), pltpu.roll(fy_m, 127, 1))
-        fy_i = jnp.where(row == 7, got(13), pltpu.roll(fy_m, 7, 0))
-        hx_y = -0.5 * ((fz_0 - fz_m) - (fy_k - fy_m))
-        hz_y = -0.5 * ((fy_i - fy_m) - (fx_0 - fx_m))
+        hx_y = -0.5 * ((fz_0 - fz_m) - (fy_k - fy_m)) * low[1]
+        fy_i = jnp.where(row == 7, 0.0, pltpu.roll(fy_m, 7, 0))
+        hz_y = -0.5 * ((fy_i - fy_m) - (fx_0 - fx_m)) * low[1]
         g_m, g_0, g_edge = got(16), send_buf[n, 17], got(14)
         gz_j = jnp.where(row == 7, g_edge, pltpu.roll(g_m, 7, 0)) - g_m
         gz_i = jnp.where(lane == 23, 0.0, pltpu.roll(g_m, 127, 1)) - g_m
         g_d = g_0 - g_m
-        h_z = -0.5 * jnp.where(
+        h_z = -0.5 * low[2] * jnp.where(
             lane < 8, g_d - pltpu.roll(gz_i, 128 - 16, 1), pltpu.roll(gz_j, 128 - 8, 1) - g_d
         )
-        new = [hy_x * low[0], hz_x * low[0], hx_y * low[1], hz_y * low[1], h_z * low[2]]
-        ghosts = new if ghosts is None else [a + b for a, b in zip(ghosts, new)]
-        hy_x, hz_x, hx_y, hz_y, h_z = ghosts
+        if n > 0:
+            hx_y, hz_y, h_z = hx_y + ghosts[2], hz_y + ghosts[3], h_z + ghosts[4]
 
         zp = got(17)
         was_owed = owed
+        owed = [None] * 5
         if n < ITERS - 1:
-            owed = [
-                lacking(lane == 0, 7, pltpu.roll(g_m, 112, 1)),
-                lacking(lane == 127, 10, pltpu.roll(zp, 120, 1)),
-                lacking(jnp.logical_and(lane == 0, row == 7), 12, pltpu.roll(g_edge, 112, 1)),
-                e_ref[2, 0],
-                pltpu.roll(e_ref[0, 7], 23, 1),
-            ]
-
-        for i in planes:
+            owed[3:] = [e_ref[2, 0], pltpu.roll(e_ref[0, 7], 23, 1)]
+
+        def update_h(i, ey_i, ez_i, which, n=n, zp=zp):
             ex, ey, ez = e_ref[0, i], e_ref[1, i], e_ref[2, i]
-            ex_j = jnp.where(row == 7, full(recv_buf[n, 21, i : i + 1, :]), pltpu.roll(ex, 7, 0))
-            ez_j = jnp.where(row == 7, full(recv_buf[n, 22, i : i + 1, :]), pltpu.roll(ez, 7, 0))
-            ex_k = jnp.where(lane == 127, full(zp[:, i : i + 1]), pltpu.roll(ex, 127, 1))
-            ey_k = jnp.where(lane == 127, full(zp[:, 8 + i : 9 + i]), pltpu.roll(ey, 127, 1))
-            ey_i = e_ref[1, i + 1] if i < 7 else ey_p
-            ez_i = e_ref[2, i + 1] if i < 7 else ez_p
-            hx = -0.5 * ((ez_j - ez) - (ey_k - ey))
-            hy = -0.5 * ((ex_k - ex) - (ez_i - ez))
-            hz = -0.5 * ((ey_i - ey) - (ex_j - ex))
-            for c, value in enumerate((hx, hy, hz)):
-                h_ref[c, i] = value if n == 0 else h_ref[c, i] + value
-
+            if 0 in which:
+                ez_j = jnp.where(
+                    row == 7, full(recv_buf[n, 22, i : i + 1, :]), pltpu.roll(ez, 7, 0)
+                )
+                ey_k = jnp.where(lane == 127, full(zp[:, 8 + i : 9 + i]), pltpu.roll(ey, 127, 1))
+                hx = -0.5 * ((ez_j - ez) - (ey_k - ey))
+                h_ref[0, i] = hx if n == 0 else h_ref[0, i] + hx
+            if 1 in which:
+                ex_j = jnp.where(
+                    row == 7, full(recv_buf[n, 21, i : i + 1, :]), pltpu.roll(ex, 7, 0)
+                )
+                ex_k = jnp.where(lane == 127, full(zp[:, i : i + 1]), pltpu.roll(ex, 127, 1))
+                hy = -0.5 * ((ex_k - ex) - (ez_i - ez))
+                hz = -0.5 * ((ey_i - ey) - (ex_j - ex))
+                h_ref[1, i] = hy if n == 0 else h_ref[1, i] + hy
+                h_ref[2, i] = hz if n == 0 else h_ref[2, i] + hz
+
+        def update_e(i, hy_i, hz_i, hx_y, hz_y, h_z, n=n):
+            hx, hy, hz = h_ref[0, i], h_ref[1, i], h_ref[2, i]
+            hx_j = jnp.where(row == 0, full(hx_y[i : i + 1, :]), pltpu.roll(hx, 1, 0))
+            hz_j = jnp.where(row == 0, full(hz_y[i : i + 1, :]), pltpu.roll(hz, 1, 0))
+            hy_k = jnp.where(lane == 0, full(h_z[:, i : i + 1]), pltpu.roll(hy, 1, 1))
+            hx_k = jnp.where(lane == 0, full(h_z[:, 8 + i : 9 + i]), pltpu.roll(hx, 1, 1))
+            rows = slice(8 * i, 8 * i + 8)
+            current = field_ref[rows, 128 * n : 128 * (n + 1)]
+            for k in range(n + 1):
+                at = ITERS + n - k
+                current = current + field_ref[rows, 128 * at : 128 * (at + 1)] * hist_ref[k, i]
+            keep_i, gain_i = keep_ref[i], gain_ref[i]
+            e_ref[0, i] = keep_i * e_ref[0, i] + gain_i * ((hz - hz_j) - (hy - hy_k))
+            e_ref[1, i] = keep_i * e_ref[1, i] + gain_i * ((hx - hx_k) - (hz - hz_i))
+            e_ref[2, i] = keep_i * e_ref[2, i] + gain_i * (((hy - hy_i) - (hx - hx_j)) - current)
+
+        for i in range(7):
+            update_h(i, e_ref[1, i + 1], e_ref[2, i + 1], (0, 1))
+        update_h(7, None, None, (0,))
         if n == 0:
             for copy in coef_copies:
                 copy.wait_recv()
             for g in range(nz):
                 gather_buf[g * cap : (g + 1) * cap, :] = coef_recv[g]
-            table = gather_buf[...]
-            spread = jnp.concatenate(
-                [
-                    jnp.where(in_lane, jnp.broadcast_to(table[:, k : k + 1], (slots, 128)), 0.0)
-                    for k in range(2 * ITERS)
-                ],
-                axis=1,
-            )
-            pieces = split(spread, 3) + [jnp.zeros(spread.shape, BF16)]
-            field_ref[...] = dot(scatter, jnp.concatenate(pieces, axis=0))
-
-        for i in planes:
-            hx, hy, hz = h_ref[0, i], h_ref[1, i], h_ref[2, i]
-            hx_j = jnp.where(row == 0, full(hx_y[i : i + 1, :]), pltpu.roll(hx, 1, 0))
-            hz_j = jnp.where(row == 0, full(hz_y[i : i + 1, :]), pltpu.roll(hz, 1, 0))
-            hy_k = jnp.where(lane == 0, full(h_z[:, i : i + 1]), pltpu.roll(hy, 1, 1))
-            hx_k = jnp.where(lane == 0, full(h_z[:, 8 + i : 9 + i]), pltpu.roll(hx, 1, 1))
-            hy_i = h_ref[1, i - 1] if i > 0 else hy_x
-            hz_i = h_ref[2, i - 1] if i > 0 else hz_x
-            rows = slice(8 * i, 8 * i + 8)
-            current = field_ref[rows, 128 * n : 128 * (n + 1)]
-            for k in range(n + 1):
-                at = ITERS + n - k
-                current = current + field_ref[rows, 128 * at : 128 * (at + 1)] * hist_ref[k, i]
-            keep, gain = keep_ref[i], gain_ref[i]
-            e_ref[0, i] = keep * e_ref[0, i] + gain * ((hz - hz_j) - (hy - hy_k))
-            e_ref[1, i] = keep * e_ref[1, i] + gain * ((hx - hx_k) - (hz - hz_i))
-            e_ref[2, i] = keep * e_ref[2, i] + gain * (((hy - hy_i) - (hx - hx_j)) - current)
+            fields(gather_buf[...], [0, ITERS])
+        e_0 = [e_ref[c, 0] for c in range(3)]
+        for i in range(1, 7):
+            update_e(i, h_ref[1, i - 1], h_ref[2, i - 1], hx_y, hz_y, h_z)
+
+        wait_recv([m for m in FAR if m not in LATE], n)
+        ex_m, ey_m, ez_m = got(4), got(5), got(6)
+        ey_p, ez_p = got(8), got(9)
+        ex_edge = got(11)
+        if n > 0:
+            ex_m, ez_p, ex_edge = ex_m + was_owed[0], ez_p + was_owed[1], ex_edge + was_owed[2]
+        update_h(7, ey_p, ez_p, (1,))
+        ex_k = jnp.where(lane == 127, 0.0, pltpu.roll(ex_m, 127, 1))
+        ex_j = jnp.where(row == 7, ex_edge, pltpu.roll(ex_m, 7, 0))
+        hy_x = -0.5 * ((ex_k - ex_m) - (e_0[2] - ez_m)) * low[0]
+        hz_x = -0.5 * ((e_0[1] - ey_m) - (ex_j - ex_m)) * low[0]
+        hz_y = hz_y - jnp.where(row == 7, 0.5 * low[1] * got(13), 0.0)
+        if n > 0:
+            hy_x, hz_x = hy_x + ghosts[0], hz_x + ghosts[1]
+        ghosts = [hy_x, hz_x, hx_y, hz_y, h_z]
+        update_e(0, hy_x, hz_x, hx_y, hz_y, h_z)
+        update_e(7, h_ref[1, 6], h_ref[2, 6], hx_y, hz_y, h_z)
 
         if n < ITERS - 1:
             pack_far(n + 1)
             send(FAR, n + 1)
+            owed[:3] = [
+                lacking(lane == 0, 7, pltpu.roll(g_m, 112, 1)),
+                lacking(lane == 127, 10, pltpu.roll(zp, 120, 1)),
+                lacking(jnp.logical_and(lane == 0, row == 7), 12, pltpu.roll(g_edge, 112, 1)),
+            ]
+        if n == 0 and ITERS > 1:
+            fields(gather_buf[...], [k for k in range(2 * ITERS) if k not in (0, ITERS)])
 
         wait_recv(LATE, n)
         x_edge, z_edge = got(0), got(2)
@@ -482,24 +549,31 @@
         e_ref[0, 7] = e_ref[0, 7] + gain_ref[7] * pltpu.roll(z_edge, 105, 1)
 
         if n < ITERS - 1:
+            if n == ITERS - 2:
+                voltages(n + 1)
+                volt_copies = send_voltages()
             pack_near(n + 1)
             send(NEAR, n + 1)
-
+            if n < ITERS - 2:
+                voltages(n + 1)
+
+    final = base_ref[...]
+    pick = first[:slots]
+    rows = [
+        jnp.where(
+            pick,
+            jnp.broadcast_to(drive[0:1], final.shape),
+            jnp.broadcast_to(drive[1:2], final.shape),
+        )
+        for drive in reversed(drives)
+    ]
     for copy in volt_copies:
         copy.wait_recv()
     for g in range(nz):
         gather_buf[g * cap : (g + 1) * cap, :] = volt_recv[g]
     table = gather_buf[...]
-    final = base_ref[...]
-    pick = first[:slots]
     for k in range(ITERS):
-        drive = drives[ITERS - 1 - k]
-        rows = jnp.where(
-            pick,
-            jnp.broadcast_to(drive[0:1], final.shape),
-            jnp.broadcast_to(drive[1:2], final.shape),
-        )
-        final = final + rows * table[:, k : k + 1]
+        final = final + rows[k] * table[:, k : k + 1]
     base_ref[...] = final
     for copy in coef_copies + volt_copies:
         copy.wait_send()
@@ -575,6 +649,8 @@
                 dma((sizes[2],)),
                 dma((sizes[2],)),
                 dma((sizes[2],)),
+                pltpu.SemaphoreType.REGULAR,
+                pltpu.SemaphoreType.REGULAR,
             ],
             compiler_params=pltpu.CompilerParams(
                 collective_id=0, has_side_effects=True, vmem_limit_bytes=32 * 1024 * 1024

time: 52.2 us -> 50.6 us (0.969)
  Pallas kernels: 51.4 us -> 49.8 us
    pallas_call x1, Pallas kernels: 50.7 us -> 49.1 us  [local(): pl.pallas_call(functools.partial(kernel, sizes), out_shape=[pltpu.VMEM(sh...]
where the time goes in v4:
time: 50.6 us; the launch traced here: 50.4 us
  Pallas kernels  49.8 us (98%)
  between operations  0.64 us (1%)
    pallas_call x1, Pallas kernels, local(): pl.pallas_call(functools.partial(kernel, sizes), out_shape=[pltpu.VMEM(sh...  49.1 us

profile of v4, /device:TPU:6, one launch (start us, length us, event | category | flops | bytes accessed | tf_op | source)
XLA Modules:
  0.0 50.4 jit_solution(3178214438457214401)
XLA Ops:
  0.6 49.1 %shard_map.130 = (f32[3,8,8,128]{3,2,1,0:T(8,128)S(1)}, f32[3,8,8,128]{3,2,1,0:T(8,128)S(1)}, f32[32,256]{1,0:T(8,128)S(1)}) custom-call(f32[3,8,8,128]{3,2,1,0:T(8,128)} %e_hbm.1, s32[8,8,128]{2,1,0:T(8,128)} %mat_hbm.1, f32[16]{0:T(128)} %eps_hbm.1, f32[16]{0:T(128)} %loss_hbm.1, s32[16]{0:T(128)} %cell_hbm.1, s32[16]{0:T(128)} %bitcast.1, s32[32]{0:T(128)} %block_hbm.1, ...), custom_call_target="tpu_custom_call" | custom-call | tf_op jit(solution)/shard_map/pallas_call | solution.py:618
  49.7 0.7 %shard_map.131 = (f32[3,8,8,128]{3,2,1,0:T(8,128)}, f32[3,8,8,128]{3,2,1,0:T(8,128)}, f32[32,256]{1,0:T(8,128)}) custom-call(f32[3,8,8,128]{3,2,1,0:T(8,128)S(1)} %get-tuple-element.6.refs_0_, f32[3,8,8,128]{3,2,1,0:T(8,128)S(1)} %get-tuple-element.7.refs_1_, f32[32,256]{1,0:T(8,128)S(1)} %get-tuple-element.8.refs_2_), custom_call_target="tpu_custom_call" | custom-call | tf_op jit(solution)/shard_map/pallas_call | solution.py:676

commit v5 on v4

--- a/solution.py
+++ b/solution.py
@@ -30,6 +30,7 @@
 TILES = 23
 LATE = (0, 1)
 FAR = range(6)
+LOW, HIGH, EDGES = (3,), (2,), (4, 5, 0, 1)
 NEAR = range(6, 12)
 
 def iota(shape, dim):
@@ -215,21 +216,27 @@
                 tile = jnp.where(lane == c * 8 + i, full(e_ref[c, i][:, k : k + 1]), tile)
         return tile
 
-    def pack_far(n):
-        e_x7, e_z0 = e_ref[0, 7], e_ref[2, 0]
-        tiles = {
-            0: pltpu.roll(e_x7, 127, 1),
-            2: pltpu.roll(e_z0, 24, 1),
-            4: e_x7,
-            5: e_ref[1, 7],
-            6: e_ref[2, 7],
-            8: e_ref[1, 0],
-            9: e_z0,
-            11: pltpu.roll(e_x7, 7, 0),
-            13: e_ref[1, 0],
-        }
+    def pack_tiles(n, tiles):
         for t, tile in tiles.items():
             send_buf[n, t] = tile
+
+    def pack_low(n):
+        pack_tiles(n, {8: e_ref[1, 0], 9: e_ref[2, 0]})
+
+    def pack_high(n):
+        pack_tiles(n, {4 + c: e_ref[c, 7] for c in range(3)})
+
+    def pack_edges(n):
+        e_x7 = e_ref[0, 7]
+        pack_tiles(
+            n,
+            {
+                0: pltpu.roll(e_x7, 127, 1),
+                2: pltpu.roll(e_ref[2, 0], 24, 1),
+                11: pltpu.roll(e_x7, 7, 0),
+                13: e_ref[1, 0],
+            },
+        )
 
     def pack_gains():
         send_buf[0, 1] = pltpu.roll(gain[7], 127, 1)
@@ -280,7 +287,9 @@
                 message(m, n).wait_send()
 
     loads[0].wait()
-    pack_far(0)
+    pack_low(0)
+    pack_high(0)
+    pack_edges(0)
     pack_gains()
     pack_near(0)
 
@@ -378,10 +387,10 @@
         def _():
             pl.semaphore_wait(faces_sem, 1)
 
-        send(FAR, 0)
+        send(LOW + HIGH + EDGES, 0)
         send(NEAR, 0)
 
-    last = me[2] >= nz - 2
+    last = me[2] >= nz - 4
     pl.when(last)(start_circuits)
     start_faces()
     pl.when(jnp.logical_not(last))(start_circuits)
@@ -504,8 +513,12 @@
                 gather_buf[g * cap : (g + 1) * cap, :] = coef_recv[g]
             fields(gather_buf[...], [0, ITERS])
         e_0 = [e_ref[c, 0] for c in range(3)]
-        for i in range(1, 7):
-            update_e(i, h_ref[1, i - 1], h_ref[2, i - 1], hx_y, hz_y, h_z)
+        def inner(n=n, hx_y=hx_y, hz_y=hz_y, h_z=h_z):
+            for i in range(1, 7):
+                update_e(i, h_ref[1, i - 1], h_ref[2, i - 1], hx_y, hz_y, h_z)
+
+        if n > 0:
+            inner()
 
         wait_recv([m for m in FAR if m not in LATE], n)
         ex_m, ey_m, ez_m = got(4), got(5), got(6)
@@ -513,26 +526,33 @@
         ex_edge = got(11)
         if n > 0:
             ex_m, ez_p, ex_edge = ex_m + was_owed[0], ez_p + was_owed[1], ex_edge + was_owed[2]
-        update_h(7, ey_p, ez_p, (1,))
         ex_k = jnp.where(lane == 127, 0.0, pltpu.roll(ex_m, 127, 1))
         ex_j = jnp.where(row == 7, ex_edge, pltpu.roll(ex_m, 7, 0))
         hy_x = -0.5 * ((ex_k - ex_m) - (e_0[2] - ez_m)) * low[0]
         hz_x = -0.5 * ((e_0[1] - ey_m) - (ex_j - ex_m)) * low[0]
-        hz_y = hz_y - jnp.where(row == 7, 0.5 * low[1] * got(13), 0.0)
         if n > 0:
             hy_x, hz_x = hy_x + ghosts[0], hz_x + ghosts[1]
+        update_e(0, hy_x, hz_x, hx_y, hz_y, h_z)
+        if n < ITERS - 1:
+            pack_low(n + 1)
+            send(LOW, n + 1)
+        update_h(7, ey_p, ez_p, (1,))
+        hz_y = hz_y - jnp.where(row == 7, 0.5 * low[1] * got(13), 0.0)
         ghosts = [hy_x, hz_x, hx_y, hz_y, h_z]
-        update_e(0, hy_x, hz_x, hx_y, hz_y, h_z)
         update_e(7, h_ref[1, 6], h_ref[2, 6], hx_y, hz_y, h_z)
 
         if n < ITERS - 1:
-            pack_far(n + 1)
-            send(FAR, n + 1)
+            pack_high(n + 1)
+            send(HIGH, n + 1)
+            pack_edges(n + 1)
+            send(EDGES, n + 1)
             owed[:3] = [
                 lacking(lane == 0, 7, pltpu.roll(g_m, 112, 1)),
                 lacking(lane == 127, 10, pltpu.roll(zp, 120, 1)),
                 lacking(jnp.logical_and(lane == 0, row == 7), 12, pltpu.roll(g_edge, 112, 1)),
             ]
+        if n == 0:
+            inner()
         if n == 0 and ITERS > 1:
             fields(gather_buf[...], [k for k in range(2 * ITERS) if k not in (0, ITERS)])
 

time: 50.6 us -> 50.1 us (level)
  Pallas kernels: 49.8 us -> 49 us
    pallas_call x1, Pallas kernels: 49.1 us -> 48.3 us  [local(): pl.pallas_call(functools.partial(kernel, sizes), out_shape=[pltpu.VMEM(sh...]
where the time goes in v5:
time: 50.1 us; the launch traced here: 49.6 us
  Pallas kernels  49 us (98%)
  between operations  0.64 us (1%)
    pallas_call x1, Pallas kernels, local(): pl.pallas_call(functools.partial(kernel, sizes), out_shape=[pltpu.VMEM(sh...  48.3 us

profile of v5, /device:TPU:6, one launch (start us, length us, event | category | flops | bytes accessed | tf_op | source)
XLA Modules:
  0.0 49.6 jit_solution(6400948695425356954)
XLA Ops:
  0.6 48.3 %shard_map.130 = (f32[3,8,8,128]{3,2,1,0:T(8,128)S(1)}, f32[3,8,8,128]{3,2,1,0:T(8,128)S(1)}, f32[32,256]{1,0:T(8,128)S(1)}) custom-call(f32[3,8,8,128]{3,2,1,0:T(8,128)} %e_hbm.1, s32[8,8,128]{2,1,0:T(8,128)} %mat_hbm.1, f32[16]{0:T(128)} %eps_hbm.1, f32[16]{0:T(128)} %loss_hbm.1, s32[16]{0:T(128)} %cell_hbm.1, s32[16]{0:T(128)} %bitcast.1, s32[32]{0:T(128)} %block_hbm.1, ...), custom_call_target="tpu_custom_call" | custom-call | tf_op jit(solution)/shard_map/pallas_call | solution.py:638
  48.9 0.7 %shard_map.131 = (f32[3,8,8,128]{3,2,1,0:T(8,128)}, f32[3,8,8,128]{3,2,1,0:T(8,128)}, f32[32,256]{1,0:T(8,128)}) custom-call(f32[3,8,8,128]{3,2,1,0:T(8,128)S(1)} %get-tuple-element.6.refs_0_, f32[3,8,8,128]{3,2,1,0:T(8,128)S(1)} %get-tuple-element.7.refs_1_, f32[32,256]{1,0:T(8,128)S(1)} %get-tuple-element.8.refs_2_), custom_call_target="tpu_custom_call" | custom-call | tf_op jit(solution)/shard_map/pallas_call | solution.py:696

commit v6 on v5

--- a/solution.py
+++ b/solution.py
@@ -145,12 +145,16 @@
         )
     ]
 
-    recv_buf[...] = jnp.zeros(recv_buf.shape, F32)
-
     barrier = pltpu.get_barrier_semaphore()
     odd = lax.rem(me[1], 2)
     is_even, is_odd = odd == 0, odd == 1
     sibling = (me[0], me[1] + 1 - 2 * odd, me[2])
+    for step in others:
+        pl.semaphore_signal(
+            barrier, inc=1, device_id=(me[0], me[1] + 1 - odd, peer(step)), device_id_type=MESH
+        )
+
+    recv_buf[...] = jnp.zeros(recv_buf.shape, F32)
     neighbours = jnp.int32(-1)
     for offset, _, _, _ in MESSAGES:
         ok = exists(offset)
@@ -168,11 +172,6 @@
                 device_id=(there[0], there[1] - lax.rem(there[1], 2), there[2]),
                 device_id_type=MESH,
             )
-
-    for step in others:
-        pl.semaphore_signal(
-            barrier, inc=1, device_id=(me[0], me[1] + 1 - odd, peer(step)), device_id_type=MESH
-        )
 
     @pl.when(is_even)
     def _():

time: 50.1 us -> 49.9 us (level)
  no operation moved by 1% of the time
where the time goes in v6:
time: 49.9 us; the launch traced here: 49.5 us
  Pallas kernels  48.9 us (98%)
  between operations  0.64 us (1%)
    pallas_call x1, Pallas kernels, local(): pl.pallas_call(functools.partial(kernel, sizes), out_shape=[pltpu.VMEM(sh...  48.1 us

profile of v6, /device:TPU:6, one launch (start us, length us, event | category | flops | bytes accessed | tf_op | source)
XLA Modules:
  0.0 49.5 jit_solution(8516124338434409134)
XLA Ops:
  0.6 48.1 %shard_map.130 = (f32[3,8,8,128]{3,2,1,0:T(8,128)S(1)}, f32[3,8,8,128]{3,2,1,0:T(8,128)S(1)}, f32[32,256]{1,0:T(8,128)S(1)}) custom-call(f32[3,8,8,128]{3,2,1,0:T(8,128)} %e_hbm.1, s32[8,8,128]{2,1,0:T(8,128)} %mat_hbm.1, f32[16]{0:T(128)} %eps_hbm.1, f32[16]{0:T(128)} %loss_hbm.1, s32[16]{0:T(128)} %cell_hbm.1, s32[16]{0:T(128)} %bitcast.1, s32[32]{0:T(128)} %block_hbm.1, ...), custom_call_target="tpu_custom_call" | custom-call | tf_op jit(solution)/shard_map/pallas_call | solution.py:637
  48.8 0.7 %shard_map.131 = (f32[3,8,8,128]{3,2,1,0:T(8,128)}, f32[3,8,8,128]{3,2,1,0:T(8,128)}, f32[32,256]{1,0:T(8,128)}) custom-call(f32[3,8,8,128]{3,2,1,0:T(8,128)S(1)} %get-tuple-element.6.refs_0_, f32[3,8,8,128]{3,2,1,0:T(8,128)S(1)} %get-tuple-element.7.refs_1_, f32[32,256]{1,0:T(8,128)S(1)} %get-tuple-element.8.refs_2_), custom_call_target="tpu_custom_call" | custom-call | tf_op jit(solution)/shard_map/pallas_call | solution.py:695
